TPU v7x, 512 devices: a whole 4x4x16 slice. The times are simulated.
512 devices in a mesh: rep: 64 (over z, x), tp: 8 (over y, core).
Axes of the slice: x: 4, y: 4, z: 16, core: 2. Of those that a mesh axis runs over, the one named last changes fastest.
Arguments:
- grads: bfloat16 [2, 64, 14336, 128], P(None, 'rep', 'tp'), may hold values from -6 to 6
- error_in: float32 [64, 14336, 128], P('rep', 'tp'), may hold values from -6 to 6
- accum_in: float32 [14336, 128], P('tp'), may hold values from -6 to 6
- picks: int32 [2, 64, 8, 2], P(None, None, 'tp'), may hold values from 0 to 1791, as said below
Outputs:
- accum_out: float32 [14336, 128], P('tp')
- error_out: float32 [64, 14336, 128], P('rep', 'tp')
Inputs may be any that keep to these rules, and one draw needn't show every extreme that they name: Each row picks[s, r, t, :] holds 2 different block numbers.
All inputs are finite; a program needn't handle non-finite values.
Results may differ from a plain program's by a relative error of at most 0.0003.
Values sent between devices are 32-bit elements; how exact they have to be, the bound alone decides.
No kernel may reach another device: no remote copies, remote signals or barrier semaphores. Data moves between devices by JAX's collectives and lax.ppermute only.
A program may use at most 64 MiB of HBM per device.

v0:
```python
import jax
import jax.numpy as jnp
from jax import lax
from jax.sharding import PartitionSpec as P

STEPS = 2


def local(grads, error_in, accum_in, picks):
    error = error_in[0]
    accum = accum_in
    blocks = error.shape[0]
    replica = lax.axis_index("rep")
    positions = jnp.arange(blocks, dtype=jnp.int32)
    for step in range(STEPS):
        corrected = grads[step, 0].astype(jnp.float32) + error
        table = picks[step, :, 0, :]
        own = lax.dynamic_index_in_dim(table, replica, 0, keepdims=False)
        chosen = jnp.any(own[:, None] == positions[None, :], axis=0)
        sent = jnp.where(chosen[:, None], corrected, jnp.float32(0.0))
        summed = lax.psum(sent, "rep")
        accum = accum + summed
        error = corrected - sent
    return (accum, error[None])


def solution(mesh):
    placed = (
        P(None, "rep", "tp", None),
        P("rep", "tp", None),
        P("tp", None),
        P(None, None, "tp", None),
    )
    return jax.shard_map(
        local,
        mesh=mesh,
        in_specs=placed,
        out_specs=(P("tp", None), P("rep", "tp", None)),
        check_vma=False,
    )
```

profile of v0, /device:TPU:24, one launch (start us, length us, event | category | flops | bytes accessed | tf_op | source)
XLA Modules:
  0.0 303.4 jit_solution(5023265028653954085)
XLA Ops:
  7.2 0.0 all-reduce.3.cloned.1.call-start
  7.2 0.0 copy-start.3
  7.2 0.7 copy-done.3
  7.9 0.2 dynamic-slice_reduce_fusion
  8.1 0.1 compare_reduce_fusion
  8.2 0.1 compare_reduce_fusion.1
  8.3 3.3 %fusion.5 = (f32[1792,128]{1,0:T(8,128)}, f32[1792,128]{1,0:T(8,128)}) fusion(f32[1,1792,128]{2,1,0:T(8,128)} %param.5, pred[1792]{0:T(1024)(128)(4,1)S(1)} %compare_reduce_fusion.1, bf16[2,1,1792,128]{3,2,1,0:T(8,128)(2,1)} %param.4, pred[1792]{0:T(1024)(128)(4,1)S(1)} %compare_reduce_fusion), kind=kLoop, calls=%fused_computation.12 | loop fusion | flops 1605632 | bytes 3673600 | tf_op jit(solution)/shard_map/jit(_where)/select_n | solution.py:20
  11.6 0.0 copy-start
  11.6 0.0 copy-start.1
  11.6 0.0 all-reduce.3.cloned.1.call-update
  11.6 1.2 copy-done
  12.8 0.3 copy-done.1
  13.1 0.0 copy-start.2
  13.1 2.3 select_subtract_fusion
  15.3 278.7 %all-reduce.3.cloned.1.call-done = (f32[1792,128]{1,0:T(8,128)}, f32[1792,128]{1,0:T(8,128)}) async-done(((f32[1792,128]{1,0:T(8,128)}, f32[1792,128]{1,0:T(8,128)}), (f32[1792,128]{1,0:T(8,128)}, f32[1792,128]{1,0:T(8,128)})) %all-reduce.3.cloned.1.call-update) | async-done | bytes 1835024 | tf_op jit(solution)/shard_map/psum | solution.py:21
  294.1 0.0 copy-done.2
  294.1 2.5 add_add_fusion
  (1 shorter events, 0.0 us)
Async XLA Ops:
  7.2 286.9 %all-reduce.3.cloned.1.call-start = ((), (), s32[]{:S(2)}) async-start(), calls=%async_computation | async-start | bytes 3670016 | tf_op jit(solution)/shard_map/psum | solution.py:21
  7.2 0.7 copy-start.3
  11.6 1.2 copy-start
  11.6 1.5 copy-start.1
  13.1 281.0 %copy-start.2 = (f32[1792,128]{1,0:T(8,128)S(1)}, f32[1792,128]{1,0:T(8,128)}, u32[]{:S(2)}) copy-start(f32[1792,128]{1,0:T(8,128)} %param.6) | copy-start | bytes 2752516
Sparse Core Ops, SparseCore 0:
  12.0 281.9 all-reduce.2
where the time goes:
time: 304 us; the launch traced here: 303 us
  waiting for transfers between devices  279 us (92%)
  between operations  14 us (5%)
  other arithmetic  8.27 us (3%)
    psum x1, waiting for transfers between devices, local(): summed = lax.psum(sent, 'rep')  279 us
  transfers between devices with their start and end apart: 1, of which 1 were waited for; matrix products, arithmetic and copies ran while one was open for 1% of the time, Pallas kernels for 0%

commit v1 on v0

v1 whole, which is shorter than its diff:
```python
import functools

import jax
import jax.numpy as jnp
from jax import lax
from jax.experimental import pallas as pl
from jax.experimental.pallas import tpu as pltpu
from jax.sharding import PartitionSpec as P

STEPS = 2
PICKS = 2
BLOCK = 128
SENT = STEPS * PICKS
FIRST = 39
F_ROWS = 8
H_ROWS = 16
KIB = 1024
ROOM = 12 * 1024 * KIB
NEARLY_ALL = (63 * 1024 + 256) * KIB


def kernel_params(limit=ROOM):
    return pltpu.CompilerParams(vmem_limit_bytes=limit)


def send_kernel(picks, grads, error, rows, halves, wholes, half_sems, whole_sems):
    replica = lax.axis_index("rep")
    chosen = [picks[j // PICKS, j % PICKS, replica] for j in range(SENT)]
    copies = []
    for j in range(SENT):
        base = pl.multiple_of((chosen[j] // F_ROWS) * F_ROWS, F_ROWS)
        copies.append(
            pltpu.make_async_copy(
                error.at[0, pl.ds(base, F_ROWS), :], wholes.at[j], whole_sems.at[j]
            )
        )
        base = pl.multiple_of((chosen[j] // H_ROWS) * H_ROWS, H_ROWS)
        for step in range(j // PICKS + 1):
            copies.append(
                pltpu.make_async_copy(
                    grads.at[step, 0, pl.ds(base, H_ROWS), :],
                    halves.at[step, j],
                    half_sems.at[step, j],
                )
            )
    for copy in copies:
        copy.start()
    for copy in copies:
        copy.wait()

    def row_of(tile, at):
        index = lax.broadcasted_iota(jnp.int32, tile.shape, 0)
        kept = jnp.where(index == at, tile, jnp.float32(0.0))
        return jnp.sum(kept, axis=0, keepdims=True)

    sent = []
    for j in range(SENT):
        at = lax.rem(chosen[j], H_ROWS)
        value = row_of(halves[0, j].astype(jnp.float32), at)
        value = value + row_of(wholes[j], lax.rem(chosen[j], F_ROWS))
        if j >= PICKS:
            again = (chosen[j] == chosen[0]) | (chosen[j] == chosen[1])
            value = jnp.where(again, jnp.float32(0.0), value)
            value = row_of(halves[1, j].astype(jnp.float32), at) + value
        sent.append(value)
    block = jnp.concatenate(sent, axis=0)
    for peer in range(rows.shape[0]):
        rows[peer] = block


def sent_rows(picks, grads, error, copies):
    return pl.pallas_call(
        send_kernel,
        out_shape=jax.ShapeDtypeStruct((copies, SENT, BLOCK), jnp.float32),
        in_specs=[
            pl.BlockSpec(memory_space=pltpu.SMEM),
            pl.BlockSpec(memory_space=pltpu.HBM),
            pl.BlockSpec(memory_space=pltpu.HBM),
        ],
        out_specs=pl.BlockSpec(memory_space=pltpu.VMEM),
        scratch_shapes=[
            pltpu.VMEM((STEPS, SENT, H_ROWS, BLOCK), jnp.bfloat16),
            pltpu.VMEM((SENT, F_ROWS, BLOCK), jnp.float32),
            pltpu.SemaphoreType.DMA((STEPS, SENT)),
            pltpu.SemaphoreType.DMA((SENT,)),
        ],
        compiler_params=kernel_params(NEARLY_ALL),
        name="sent_rows",
    )(picks, grads, error)


def error_kernel(head, picks, table, grads, error, out, hot):
    replica = lax.axis_index("rep")
    size = out.shape[1]
    first = pl.program_id(0) * size
    index = lax.broadcasted_iota(jnp.int32, (size, BLOCK), 0) + first
    value = error[0]
    for step in range(STEPS):
        value = grads[step, 0].astype(jnp.float32) + value
        for k in range(PICKS):
            value = jnp.where(index == picks[step, k, replica], jnp.float32(0.0), value)
    out[0] = value
    lanes = []
    for j in range(SENT):
        lane = table[j // PICKS, pl.ds(j % PICKS, 1), :]
        lanes += [lane[:, head:], lane[:, :head]]
    order = jnp.concatenate(lanes, axis=1)
    index = lax.broadcasted_iota(jnp.int32, hot.shape, 0) + first
    hits = jnp.where(index == order, jnp.float32(1.0), jnp.float32(0.0))
    hot[...] = hits.astype(jnp.bfloat16)


def next_error(head, picks, grads, error, tiles=4):
    blocks = error.shape[1]
    size = blocks // tiles
    count = SENT * picks.shape[2]
    return pl.pallas_call(
        functools.partial(error_kernel, head),
        grid=(tiles,),
        out_shape=(
            jax.ShapeDtypeStruct(error.shape, jnp.float32),
            jax.ShapeDtypeStruct((blocks, count), jnp.bfloat16),
        ),
        in_specs=[
            pl.BlockSpec(memory_space=pltpu.SMEM),
            pl.BlockSpec(picks.shape, lambda i: (0, 0, 0)),
            pl.BlockSpec((STEPS, 1, size, BLOCK), lambda i: (0, 0, i, 0)),
            pl.BlockSpec((1, size, BLOCK), lambda i: (0, i, 0)),
        ],
        out_specs=(
            pl.BlockSpec((1, size, BLOCK), lambda i: (0, i, 0)),
            pl.BlockSpec((size, count), lambda i: (i, 0)),
        ),
        compiler_params=kernel_params(),
        cost_estimate=pl.CostEstimate(
            flops=8 * error.size, bytes_accessed=16 * error.size, transcendentals=0
        ),
        name="next_error",
    )(picks, picks, grads, error)


def add_kernel(hot, rows, accum, out, sums, sems):
    count = rows.shape[0] // SENT
    value = jnp.concatenate(
        [rows[pl.ds(j, count, SENT), :] for j in range(SENT)], axis=0
    )
    high = value.astype(jnp.bfloat16)
    rest = value - high.astype(jnp.float32)
    middle = rest.astype(jnp.bfloat16)
    low = (rest - middle.astype(jnp.float32)).astype(jnp.bfloat16)
    pair = jnp.concatenate([high, middle], axis=1)
    tiles = sems.shape[0]
    size = accum.shape[0] // tiles
    copies = []
    for tile in range(tiles):
        part = pl.ds(tile * size, size)
        both = jnp.dot(hot[part, :], pair, preferred_element_type=jnp.float32)
        small = jnp.dot(hot[part, :], low, preferred_element_type=jnp.float32)
        total = both[:, :BLOCK] + (both[:, BLOCK:] + small)
        sums[part, :] = accum[part, :] + total
        copy = pltpu.make_async_copy(sums.at[part, :], out.at[part, :], sems.at[tile])
        copy.start()
        copies.append(copy)
    for copy in copies:
        copy.wait()


def add_rows(hot, rows, accum, tiles=7):
    return pl.pallas_call(
        add_kernel,
        out_shape=jax.ShapeDtypeStruct(accum.shape, jnp.float32),
        in_specs=[pl.BlockSpec(memory_space=pltpu.VMEM)] * 3,
        out_specs=pl.BlockSpec(memory_space=pltpu.HBM),
        scratch_shapes=[
            pltpu.VMEM(accum.shape, jnp.float32),
            pltpu.SemaphoreType.DMA((tiles,)),
        ],
        compiler_params=kernel_params(),
        name="add_rows",
    )(hot, rows, accum)


def local(grads, error_in, accum_in, picks):
    table = jnp.swapaxes(picks[:, :, 0, :], 1, 2)
    count = lax.axis_size("rep")
    first = FIRST
    members = [(first + r) % count for r in range(count)]
    rows = sent_rows(table, grads, error_in, count)
    rows = lax.all_to_all(
        rows, "rep", 0, 0, axis_index_groups=[members], tiled=True
    )
    error, hot = next_error(first, table, grads, error_in)
    rows = rows.reshape(count * SENT, BLOCK)
    return (add_rows(hot, rows, accum_in), error)


def solution(mesh):
    placed = (
        P(None, "rep", "tp", None),
        P("rep", "tp", None),
        P("tp", None),
        P(None, None, "tp", None),
    )
    return jax.shard_map(
        local,
        mesh=mesh,
        in_specs=placed,
        out_specs=(P("tp", None), P("rep", "tp", None)),
        check_vma=False,
    )
```

time: 304 us -> 34 us (0.11)
  waiting for transfers between devices: 279 us -> 2.89 us
  starting transfers between devices: 0.04 us -> 21.6 us
  between operations: 14 us -> 0.67 us
  other arithmetic: 8.27 us -> 0 us
  Pallas kernels: 0 us -> 6.19 us
    psum x1 -> x0, waiting for transfers between devices: 279 us -> none  [local(): summed = lax.psum(sent, 'rep')]
    all_to_all x0 -> x1, starting transfers between devices: none -> 21.6 us  [local(): lax.all_to_all(rows, 'rep', 0, 0, axis_index_groups=[members], tiled=True)]
    pallas_call x0 -> x3, Pallas kernels: none -> 6.19 us  [the longest x1 2.48 us: next_error(): pl.pallas_call(functools.partial(error_kernel, head), grid=(tiles,), out_...]
    select_n x1 -> x0, other arithmetic: 3.29 us -> none  [local(): sent = jnp.where(chosen[:, None], corrected, jnp.float32(0.0))]
  transfers between devices with their start and end apart: 1 -> 1, of which waited for: 1 -> 1; matrix products, arithmetic and copies ran while one was open for 1% -> 0% of each run, Pallas kernels for 0% -> 7%
where the time goes in v1:
time: 34 us; the launch traced here: 33.7 us
  starting transfers between devices  21.6 us (64%)
  Pallas kernels  6.19 us (18%)
  waiting for transfers between devices  2.89 us (8%)
  local copies, waits for them, and re-layouts  2.36 us (7%)
  between operations  0.67 us (2%)
    all_to_all x1, starting transfers between devices, local(): lax.all_to_all(rows, 'rep', 0, 0, axis_index_groups=[members], tiled=True)  21.6 us
    all_to_all x1, waiting for transfers between devices, local(): lax.all_to_all(rows, 'rep', 0, 0, axis_index_groups=[members], tiled=True)  2.89 us
    pallas_call x1, Pallas kernels, next_error(): pl.pallas_call(functools.partial(error_kernel, head), grid=(tiles,), out_...  2.48 us
    unnamed x8, local copies, waits for them, and re-layouts  2.36 us
    pallas_call x1, Pallas kernels, sent_rows(): pl.pallas_call(send_kernel, out_shape=jax.ShapeDtypeStruct((copies, SENT,...  2.34 us
    pallas_call x1, Pallas kernels, add_rows(): pl.pallas_call(add_kernel, out_shape=jax.ShapeDtypeStruct(accum.shape, jn...  1.37 us
  transfers between devices with their start and end apart: 1, of which 1 were waited for; matrix products, arithmetic and copies ran while one was open for 0% of the time, Pallas kernels for 7%

profile of v1, /device:TPU:24, one launch (start us, length us, event | category | flops | bytes accessed | tf_op | source)
XLA Modules:
  0.0 33.7 jit_solution(535408807896091670)
XLA Ops:
  0.6 2.3 %sent_rows.1 = f32[64,4,128]{2,1,0:T(4,128)} custom-call(s32[2,2,64]{2,1,0:T(2,128)} %bitcast.5, bf16[2,1,1792,128]{3,2,1,0:T(8,128)(2,1)} %grads.3, f32[1,1792,128]{2,1,0:T(8,128)} %error.3), custom_call_target="tpu_custom_call" | custom-call | tf_op jit(solution)/shard_map/sent_rows/pallas_call | solution.py:72
  3.0 0.0 copy-start.3
  3.0 21.6 %all-to-all-start = ((f32[64,4,128]{2,1,0:T(4,128)}), f32[64,4,128]{2,1,0:T(4,128)S(1)}, u32[]{:S(2)}, u32[]{:S(2)}) async-start(f32[64,4,128]{2,1,0:T(4,128)} %sent_rows.1), calls=%async_computation | async-start | bytes 262144 | tf_op jit(solution)/shard_map/all_to_all | solution.py:189
  24.6 0.0 copy-done.3
  24.6 0.0 copy-start
  24.6 1.2 %copy-done = bf16[2,1,1792,128]{3,2,1,0:T(8,128)(2,1)S(1)} copy-done((bf16[2,1,1792,128]{3,2,1,0:T(8,128)(2,1)S(1)}, bf16[2,1,1792,128]{3,2,1,0:T(8,128)(2,1)}, u32[]{:S(2)}) %copy-start) | copy-done | bytes 917528
  25.8 0.0 copy-start.1
  25.8 1.2 %copy-done.1 = f32[1,1792,128]{2,1,0:T(8,128)S(1)} copy-done((f32[1,1792,128]{2,1,0:T(8,128)S(1)}, f32[1,1792,128]{2,1,0:T(8,128)}, u32[]{:S(2)}) %copy-start.1) | copy-done | bytes 917528
  27.0 0.0 copy-start.2
  27.0 2.5 %next_error.1 = (f32[1,1792,128]{2,1,0:T(8,128)}, bf16[1792,256]{1,0:T(8,128)(2,1)S(1)}) custom-call(s32[2,2,64]{2,1,0:T(2,128)S(1)} %bitcast.6, s32[2,2,64]{2,1,0:T(2,128)S(1)} %bitcast.7, bf16[2,1,1792,128]{3,2,1,0:T(8,128)(2,1)S(1)} %copy-done, f32[1,1792,128]{2,1,0:T(8,128)S(1)} %copy-done.1), custom_call_target="tpu_custom_call" | custom-call | flops 1835008 | bytes 3670016 | tf_op jit(solution)/shard_map/next_error/pallas_call | solution.py:117
  29.5 2.9 %all-to-all-done = f32[64,4,128]{2,1,0:T(4,128)S(1)} async-done(((f32[64,4,128]{2,1,0:T(4,128)}), f32[64,4,128]{2,1,0:T(4,128)S(1)}, u32[]{:S(2)}, u32[]{:S(2)}) %all-to-all-start) | async-done | bytes 131104 | tf_op jit(solution)/shard_map/all_to_all | solution.py:189
  32.3 0.0 copy-done.2
  32.3 1.4 %add_rows.1 = f32[1792,128]{1,0:T(8,128)} custom-call(bf16[1792,256]{1,0:T(8,128)(2,1)S(1)} %get-tuple-element.4.hot, f32[256,128]{1,0:T(8,128)S(1)} %bitcast.4, f32[1792,128]{1,0:T(8,128)S(1)} %copy-done.2), custom_call_target="tpu_custom_call" | custom-call | tf_op jit(solution)/shard_map/add_rows/pallas_call | solution.py:169
Async XLA Ops:
  3.0 21.6 %copy-start.3 = (s32[2,64,1,2]{1,3,2,0:T(2,128)S(1)}, s32[2,64,1,2]{1,3,2,0:T(2,128)}, u32[]{:S(2)}) copy-start(s32[2,64,1,2]{1,3,2,0:T(2,128)} %param.7) | copy-start | bytes 3076
  3.0 29.4 %all-to-all-start = ((f32[64,4,128]{2,1,0:T(4,128)}), f32[64,4,128]{2,1,0:T(4,128)S(1)}, u32[]{:S(2)}, u32[]{:S(2)}) async-start(f32[64,4,128]{2,1,0:T(4,128)} %sent_rows.1), calls=%async_computation | async-start | bytes 262144 | tf_op jit(solution)/shard_map/all_to_all | solution.py:189
  24.6 1.2 %copy-start = (bf16[2,1,1792,128]{3,2,1,0:T(8,128)(2,1)S(1)}, bf16[2,1,1792,128]{3,2,1,0:T(8,128)(2,1)}, u32[]{:S(2)}) copy-start(bf16[2,1,1792,128]{3,2,1,0:T(8,128)(2,1)} %grads.3) | copy-start | bytes 2752516
  25.8 1.2 %copy-start.1 = (f32[1,1792,128]{2,1,0:T(8,128)S(1)}, f32[1,1792,128]{2,1,0:T(8,128)}, u32[]{:S(2)}) copy-start(f32[1,1792,128]{2,1,0:T(8,128)} %error.3) | copy-start | bytes 2752516
  27.0 5.4 %copy-start.2 = (f32[1792,128]{1,0:T(8,128)S(1)}, f32[1792,128]{1,0:T(8,128)}, u32[]{:S(2)}) copy-start(f32[1792,128]{1,0:T(8,128)} %accum.1) | copy-start | bytes 2752516

commit v2 on v1

--- a/solution.py
+++ b/solution.py
@@ -11,7 +11,10 @@
 PICKS = 2
 BLOCK = 128
 SENT = STEPS * PICKS
-FIRST = 39
+WIDE = 4
+FIRST_Z = 9
+FIRST_X = 3
+EARLY_Z = 1
 F_ROWS = 8
 H_ROWS = 16
 KIB = 1024
@@ -35,14 +38,14 @@
             )
         )
         base = pl.multiple_of((chosen[j] // H_ROWS) * H_ROWS, H_ROWS)
-        for step in range(j // PICKS + 1):
-            copies.append(
-                pltpu.make_async_copy(
-                    grads.at[step, 0, pl.ds(base, H_ROWS), :],
-                    halves.at[step, j],
-                    half_sems.at[step, j],
-                )
+        steps = pl.ds(0, j // PICKS + 1)
+        copies.append(
+            pltpu.make_async_copy(
+                grads.at[steps, 0, pl.ds(base, H_ROWS), :],
+                halves.at[j, steps],
+                half_sems.at[j],
             )
+        )
     for copy in copies:
         copy.start()
     for copy in copies:
@@ -56,12 +59,12 @@
     sent = []
     for j in range(SENT):
         at = lax.rem(chosen[j], H_ROWS)
-        value = row_of(halves[0, j].astype(jnp.float32), at)
+        value = row_of(halves[j, 0].astype(jnp.float32), at)
         value = value + row_of(wholes[j], lax.rem(chosen[j], F_ROWS))
         if j >= PICKS:
             again = (chosen[j] == chosen[0]) | (chosen[j] == chosen[1])
             value = jnp.where(again, jnp.float32(0.0), value)
-            value = row_of(halves[1, j].astype(jnp.float32), at) + value
+            value = row_of(halves[j, 1].astype(jnp.float32), at) + value
         sent.append(value)
     block = jnp.concatenate(sent, axis=0)
     for peer in range(rows.shape[0]):
@@ -79,9 +82,9 @@
         ],
         out_specs=pl.BlockSpec(memory_space=pltpu.VMEM),
         scratch_shapes=[
-            pltpu.VMEM((STEPS, SENT, H_ROWS, BLOCK), jnp.bfloat16),
+            pltpu.VMEM((SENT, STEPS, H_ROWS, BLOCK), jnp.bfloat16),
             pltpu.VMEM((SENT, F_ROWS, BLOCK), jnp.float32),
-            pltpu.SemaphoreType.DMA((STEPS, SENT)),
+            pltpu.SemaphoreType.DMA((SENT,)),
             pltpu.SemaphoreType.DMA((SENT,)),
         ],
         compiler_params=kernel_params(NEARLY_ALL),
@@ -89,7 +92,7 @@
     )(picks, grads, error)
 
 
-def error_kernel(head, picks, table, grads, error, out, hot):
+def error_kernel(picks, table, grads, error, out, hot):
     replica = lax.axis_index("rep")
     size = out.shape[1]
     first = pl.program_id(0) * size
@@ -100,22 +103,20 @@
         for k in range(PICKS):
             value = jnp.where(index == picks[step, k, replica], jnp.float32(0.0), value)
     out[0] = value
-    lanes = []
-    for j in range(SENT):
-        lane = table[j // PICKS, pl.ds(j % PICKS, 1), :]
-        lanes += [lane[:, head:], lane[:, :head]]
-    order = jnp.concatenate(lanes, axis=1)
+    order = jnp.concatenate(
+        [table[j // PICKS, pl.ds(j % PICKS, 1), :] for j in range(SENT)], axis=1
+    )
     index = lax.broadcasted_iota(jnp.int32, hot.shape, 0) + first
     hits = jnp.where(index == order, jnp.float32(1.0), jnp.float32(0.0))
     hot[...] = hits.astype(jnp.bfloat16)
 
 
-def next_error(head, picks, grads, error, tiles=4):
+def next_error(picks, grads, error, tiles=4):
     blocks = error.shape[1]
     size = blocks // tiles
     count = SENT * picks.shape[2]
     return pl.pallas_call(
-        functools.partial(error_kernel, head),
+        error_kernel,
         grid=(tiles,),
         out_shape=(
             jax.ShapeDtypeStruct(error.shape, jnp.float32),
@@ -139,11 +140,11 @@
     )(picks, picks, grads, error)
 
 
-def add_kernel(hot, rows, accum, out, sums, sems):
-    count = rows.shape[0] // SENT
-    value = jnp.concatenate(
-        [rows[pl.ds(j, count, SENT), :] for j in range(SENT)], axis=0
-    )
+def add_kernel(members, hot, rows, accum, out, turned, sums, sems):
+    count = len(members)
+    for place, replica in enumerate(members):
+        turned[pl.ds(replica, SENT, count), :] = rows[pl.ds(place * SENT, SENT), :]
+    value = turned[...]
     high = value.astype(jnp.bfloat16)
     rest = value - high.astype(jnp.float32)
     middle = rest.astype(jnp.bfloat16)
@@ -165,13 +166,14 @@
         copy.wait()
 
 
-def add_rows(hot, rows, accum, tiles=7):
+def add_rows(members, hot, rows, accum, tiles=7):
     return pl.pallas_call(
-        add_kernel,
+        functools.partial(add_kernel, members),
         out_shape=jax.ShapeDtypeStruct(accum.shape, jnp.float32),
         in_specs=[pl.BlockSpec(memory_space=pltpu.VMEM)] * 3,
         out_specs=pl.BlockSpec(memory_space=pltpu.HBM),
         scratch_shapes=[
+            pltpu.VMEM(rows.shape, jnp.float32),
             pltpu.VMEM(accum.shape, jnp.float32),
             pltpu.SemaphoreType.DMA((tiles,)),
         ],
@@ -180,18 +182,28 @@
     )(hot, rows, accum)
 
 
+def exchange_order(count):
+    deep = count // WIDE
+    first = FIRST_Z * WIDE + FIRST_X
+    members = [first]
+    for step in range(deep):
+        z = (step // 2 + 1) % deep if step % 2 else (deep - step // 2) % deep
+        z = (z + EARLY_Z) % deep
+        members += [z * WIDE + x for x in range(WIDE) if z * WIDE + x != first]
+    return members
+
+
 def local(grads, error_in, accum_in, picks):
     table = jnp.swapaxes(picks[:, :, 0, :], 1, 2)
     count = lax.axis_size("rep")
-    first = FIRST
-    members = [(first + r) % count for r in range(count)]
+    members = exchange_order(count)
     rows = sent_rows(table, grads, error_in, count)
     rows = lax.all_to_all(
         rows, "rep", 0, 0, axis_index_groups=[members], tiled=True
     )
-    error, hot = next_error(first, table, grads, error_in)
+    error, hot = next_error(table, grads, error_in)
     rows = rows.reshape(count * SENT, BLOCK)
-    return (add_rows(hot, rows, accum_in), error)
+    return (add_rows(members, hot, rows, accum_in), error)
 
 
 def solution(mesh):

time: 34 us -> 34.1 us (level)
  no operation moved by 1% of the time
where the time goes in v2:
time: 34.1 us; the launch traced here: 33.8 us
  starting transfers between devices  21.5 us (63%)
  Pallas kernels  6.2 us (18%)
  waiting for transfers between devices  3.03 us (9%)
  local copies, waits for them, and re-layouts  2.36 us (7%)
  between operations  0.67 us (2%)
    all_to_all x1, starting transfers between devices, local(): lax.all_to_all(rows, 'rep', 0, 0, axis_index_groups=[members], tiled=True)  21.5 us
    all_to_all x1, waiting for transfers between devices, local(): lax.all_to_all(rows, 'rep', 0, 0, axis_index_groups=[members], tiled=True)  3.03 us
    pallas_call x1, Pallas kernels, next_error(): pl.pallas_call(error_kernel, grid=(tiles,), out_shape=(jax.ShapeDtypeStru...  2.47 us
    unnamed x8, local copies, waits for them, and re-layouts  2.36 us
    pallas_call x1, Pallas kernels, sent_rows(): pl.pallas_call(send_kernel, out_shape=jax.ShapeDtypeStruct((copies, SENT,...  2.28 us
    pallas_call x1, Pallas kernels, add_rows(): pl.pallas_call(functools.partial(add_kernel, members), out_shape=jax.Shap...  1.44 us
  transfers between devices with their start and end apart: 1, of which 1 were waited for; matrix products, arithmetic and copies ran while one was open for 0% of the time, Pallas kernels for 7%

profile of v2, /device:TPU:24, one launch (start us, length us, event | category | flops | bytes accessed | tf_op | source)
XLA Modules:
  0.0 33.8 jit_solution(2287983597599314496)
XLA Ops:
  0.6 2.3 %sent_rows.1 = f32[64,4,128]{2,1,0:T(4,128)} custom-call(s32[2,2,64]{2,1,0:T(2,128)} %bitcast.5, bf16[2,1,1792,128]{3,2,1,0:T(8,128)(2,1)} %grads.3, f32[1,1792,128]{2,1,0:T(8,128)} %error.3), custom_call_target="tpu_custom_call" | custom-call | tf_op jit(solution)/shard_map/sent_rows/pallas_call | solution.py:75
  2.9 0.0 copy-start.3
  2.9 21.5 %all-to-all-start = ((f32[64,4,128]{2,1,0:T(4,128)}), f32[64,4,128]{2,1,0:T(4,128)S(1)}, u32[]{:S(2)}, u32[]{:S(2)}) async-start(f32[64,4,128]{2,1,0:T(4,128)} %sent_rows.1), calls=%async_computation | async-start | bytes 262144 | tf_op jit(solution)/shard_map/all_to_all | solution.py:201
  24.5 0.0 copy-done.3
  24.5 0.0 copy-start
  24.5 1.2 %copy-done = bf16[2,1,1792,128]{3,2,1,0:T(8,128)(2,1)S(1)} copy-done((bf16[2,1,1792,128]{3,2,1,0:T(8,128)(2,1)S(1)}, bf16[2,1,1792,128]{3,2,1,0:T(8,128)(2,1)}, u32[]{:S(2)}) %copy-start) | copy-done | bytes 917528
  25.7 0.0 copy-start.1
  25.7 1.2 %copy-done.1 = f32[1,1792,128]{2,1,0:T(8,128)S(1)} copy-done((f32[1,1792,128]{2,1,0:T(8,128)S(1)}, f32[1,1792,128]{2,1,0:T(8,128)}, u32[]{:S(2)}) %copy-start.1) | copy-done | bytes 917528
  26.9 0.0 copy-start.2
  26.9 2.5 %next_error.1 = (f32[1,1792,128]{2,1,0:T(8,128)}, bf16[1792,256]{1,0:T(8,128)(2,1)S(1)}) custom-call(s32[2,2,64]{2,1,0:T(2,128)S(1)} %bitcast.6, s32[2,2,64]{2,1,0:T(2,128)S(1)} %bitcast.7, bf16[2,1,1792,128]{3,2,1,0:T(8,128)(2,1)S(1)} %copy-done, f32[1,1792,128]{2,1,0:T(8,128)S(1)} %copy-done.1), custom_call_target="tpu_custom_call" | custom-call | flops 1835008 | bytes 3670016 | tf_op jit(solution)/shard_map/next_error/pallas_call | solution.py:118
  29.3 3.0 %all-to-all-done = f32[64,4,128]{2,1,0:T(4,128)S(1)} async-done(((f32[64,4,128]{2,1,0:T(4,128)}), f32[64,4,128]{2,1,0:T(4,128)S(1)}, u32[]{:S(2)}, u32[]{:S(2)}) %all-to-all-start) | async-done | bytes 131104 | tf_op jit(solution)/shard_map/all_to_all | solution.py:201
  32.4 0.0 copy-done.2
  32.4 1.4 %add_rows.1 = f32[1792,128]{1,0:T(8,128)} custom-call(bf16[1792,256]{1,0:T(8,128)(2,1)S(1)} %get-tuple-element.4.hot, f32[256,128]{1,0:T(8,128)S(1)} %bitcast.4, f32[1792,128]{1,0:T(8,128)S(1)} %copy-done.2), custom_call_target="tpu_custom_call" | custom-call | tf_op jit(solution)/shard_map/add_rows/pallas_call | solution.py:170
Async XLA Ops:
  2.9 21.6 %copy-start.3 = (s32[2,64,1,2]{1,3,2,0:T(2,128)S(1)}, s32[2,64,1,2]{1,3,2,0:T(2,128)}, u32[]{:S(2)}) copy-start(s32[2,64,1,2]{1,3,2,0:T(2,128)} %param.7) | copy-start | bytes 3076
  2.9 29.4 %all-to-all-start = ((f32[64,4,128]{2,1,0:T(4,128)}), f32[64,4,128]{2,1,0:T(4,128)S(1)}, u32[]{:S(2)}, u32[]{:S(2)}) async-start(f32[64,4,128]{2,1,0:T(4,128)} %sent_rows.1), calls=%async_computation | async-start | bytes 262144 | tf_op jit(solution)/shard_map/all_to_all | solution.py:201
  24.5 1.2 %copy-start = (bf16[2,1,1792,128]{3,2,1,0:T(8,128)(2,1)S(1)}, bf16[2,1,1792,128]{3,2,1,0:T(8,128)(2,1)}, u32[]{:S(2)}) copy-start(bf16[2,1,1792,128]{3,2,1,0:T(8,128)(2,1)} %grads.3) | copy-start | bytes 2752516
  25.7 1.2 %copy-start.1 = (f32[1,1792,128]{2,1,0:T(8,128)S(1)}, f32[1,1792,128]{2,1,0:T(8,128)}, u32[]{:S(2)}) copy-start(f32[1,1792,128]{2,1,0:T(8,128)} %error.3) | copy-start | bytes 2752516
  26.9 5.5 %copy-start.2 = (f32[1792,128]{1,0:T(8,128)S(1)}, f32[1792,128]{1,0:T(8,128)}, u32[]{:S(2)}) copy-start(f32[1792,128]{1,0:T(8,128)} %accum.1) | copy-start | bytes 2752516

commit v3 on v2

--- a/solution.py
+++ b/solution.py
@@ -12,9 +12,8 @@
 BLOCK = 128
 SENT = STEPS * PICKS
 WIDE = 4
-FIRST_Z = 9
-FIRST_X = 3
-EARLY_Z = 1
+FIRST_Z = 11
+FIRST_X = 1
 F_ROWS = 8
 H_ROWS = 16
 KIB = 1024
@@ -146,19 +145,15 @@
         turned[pl.ds(replica, SENT, count), :] = rows[pl.ds(place * SENT, SENT), :]
     value = turned[...]
     high = value.astype(jnp.bfloat16)
-    rest = value - high.astype(jnp.float32)
-    middle = rest.astype(jnp.bfloat16)
-    low = (rest - middle.astype(jnp.float32)).astype(jnp.bfloat16)
-    pair = jnp.concatenate([high, middle], axis=1)
+    low = (value - high.astype(jnp.float32)).astype(jnp.bfloat16)
+    pair = jnp.concatenate([high, low], axis=1)
     tiles = sems.shape[0]
     size = accum.shape[0] // tiles
     copies = []
     for tile in range(tiles):
         part = pl.ds(tile * size, size)
         both = jnp.dot(hot[part, :], pair, preferred_element_type=jnp.float32)
-        small = jnp.dot(hot[part, :], low, preferred_element_type=jnp.float32)
-        total = both[:, :BLOCK] + (both[:, BLOCK:] + small)
-        sums[part, :] = accum[part, :] + total
+        sums[part, :] = accum[part, :] + (both[:, :BLOCK] + both[:, BLOCK:])
         copy = pltpu.make_async_copy(sums.at[part, :], out.at[part, :], sems.at[tile])
         copy.start()
         copies.append(copy)
@@ -183,14 +178,8 @@
 
 
 def exchange_order(count):
-    deep = count // WIDE
     first = FIRST_Z * WIDE + FIRST_X
-    members = [first]
-    for step in range(deep):
-        z = (step // 2 + 1) % deep if step % 2 else (deep - step // 2) % deep
-        z = (z + EARLY_Z) % deep
-        members += [z * WIDE + x for x in range(WIDE) if z * WIDE + x != first]
-    return members
+    return [(first + place) % count for place in range(count)]
 
 
 def local(grads, error_in, accum_in, picks):

time: 34.1 us -> 34 us (level)
  waiting for transfers between devices: 3.03 us -> 5.38 us
  starting transfers between devices: 21.5 us -> 19.2 us
    all_to_all x1, waiting for transfers between devices: 3.03 us -> 5.38 us  [local(): lax.all_to_all(rows, 'rep', 0, 0, axis_index_groups=[members], tiled=True)]
    all_to_all x1, starting transfers between devices: 21.5 us -> 19.2 us  [local(): lax.all_to_all(rows, 'rep', 0, 0, axis_index_groups=[members], tiled=True)]
where the time goes in v3:
time: 34 us; the launch traced here: 33.7 us
  starting transfers between devices  19.2 us (56%)
  Pallas kernels  6.05 us (18%)
  waiting for transfers between devices  5.38 us (16%)
  local copies, waits for them, and re-layouts  2.36 us (7%)
  between operations  0.67 us (2%)
    all_to_all x1, starting transfers between devices, local(): lax.all_to_all(rows, 'rep', 0, 0, axis_index_groups=[members], tiled=True)  19.2 us
    all_to_all x1, waiting for transfers between devices, local(): lax.all_to_all(rows, 'rep', 0, 0, axis_index_groups=[members], tiled=True)  5.38 us
    pallas_call x1, Pallas kernels, next_error(): pl.pallas_call(error_kernel, grid=(tiles,), out_shape=(jax.ShapeDtypeStru...  2.47 us
    unnamed x8, local copies, waits for them, and re-layouts  2.36 us
    pallas_call x1, Pallas kernels, sent_rows(): pl.pallas_call(send_kernel, out_shape=jax.ShapeDtypeStruct((copies, SENT,...  2.28 us
    pallas_call x1, Pallas kernels, add_rows(): pl.pallas_call(functools.partial(add_kernel, members), out_shape=jax.Shap...  1.29 us
  transfers between devices with their start and end apart: 1, of which 1 were waited for; matrix products, arithmetic and copies ran while one was open for 0% of the time, Pallas kernels for 7%

profile of v3, /device:TPU:24, one launch (start us, length us, event | category | flops | bytes accessed | tf_op | source)
XLA Modules:
  0.0 33.7 jit_solution(4743687217038821933)
XLA Ops:
  0.6 2.3 %sent_rows.1 = f32[64,4,128]{2,1,0:T(4,128)} custom-call(s32[2,2,64]{2,1,0:T(2,128)} %bitcast.5, bf16[2,1,1792,128]{3,2,1,0:T(8,128)(2,1)} %grads.3, f32[1,1792,128]{2,1,0:T(8,128)} %error.3), custom_call_target="tpu_custom_call" | custom-call | tf_op jit(solution)/shard_map/sent_rows/pallas_call | solution.py:74
  2.9 0.0 copy-start.3
  2.9 19.2 %all-to-all-start = ((f32[64,4,128]{2,1,0:T(4,128)}), f32[64,4,128]{2,1,0:T(4,128)S(1)}, u32[]{:S(2)}, u32[]{:S(2)}) async-start(f32[64,4,128]{2,1,0:T(4,128)} %sent_rows.1), calls=%async_computation | async-start | bytes 262144 | tf_op jit(solution)/shard_map/all_to_all | solution.py:190
  22.1 0.0 copy-done.3
  22.2 0.0 copy-start
  22.2 1.2 %copy-done = bf16[2,1,1792,128]{3,2,1,0:T(8,128)(2,1)S(1)} copy-done((bf16[2,1,1792,128]{3,2,1,0:T(8,128)(2,1)S(1)}, bf16[2,1,1792,128]{3,2,1,0:T(8,128)(2,1)}, u32[]{:S(2)}) %copy-start) | copy-done | bytes 917528
  23.3 0.0 copy-start.1
  23.3 1.2 %copy-done.1 = f32[1,1792,128]{2,1,0:T(8,128)S(1)} copy-done((f32[1,1792,128]{2,1,0:T(8,128)S(1)}, f32[1,1792,128]{2,1,0:T(8,128)}, u32[]{:S(2)}) %copy-start.1) | copy-done | bytes 917528
  24.5 0.0 copy-start.2
  24.5 2.5 %next_error.1 = (f32[1,1792,128]{2,1,0:T(8,128)}, bf16[1792,256]{1,0:T(8,128)(2,1)S(1)}) custom-call(s32[2,2,64]{2,1,0:T(2,128)S(1)} %bitcast.6, s32[2,2,64]{2,1,0:T(2,128)S(1)} %bitcast.7, bf16[2,1,1792,128]{3,2,1,0:T(8,128)(2,1)S(1)} %copy-done, f32[1,1792,128]{2,1,0:T(8,128)S(1)} %copy-done.1), custom_call_target="tpu_custom_call" | custom-call | flops 1835008 | bytes 3670016 | tf_op jit(solution)/shard_map/next_error/pallas_call | solution.py:117
  27.0 5.4 %all-to-all-done = f32[64,4,128]{2,1,0:T(4,128)S(1)} async-done(((f32[64,4,128]{2,1,0:T(4,128)}), f32[64,4,128]{2,1,0:T(4,128)S(1)}, u32[]{:S(2)}, u32[]{:S(2)}) %all-to-all-start) | async-done | bytes 131104 | tf_op jit(solution)/shard_map/all_to_all | solution.py:190
  32.4 0.0 copy-done.2
  32.4 1.3 %add_rows.1 = f32[1792,128]{1,0:T(8,128)} custom-call(bf16[1792,256]{1,0:T(8,128)(2,1)S(1)} %get-tuple-element.4.hot, f32[256,128]{1,0:T(8,128)S(1)} %bitcast.4, f32[1792,128]{1,0:T(8,128)S(1)} %copy-done.2), custom_call_target="tpu_custom_call" | custom-call | tf_op jit(solution)/shard_map/add_rows/pallas_call | solution.py:165
Async XLA Ops:
  2.9 19.2 %copy-start.3 = (s32[2,64,1,2]{1,3,2,0:T(2,128)S(1)}, s32[2,64,1,2]{1,3,2,0:T(2,128)}, u32[]{:S(2)}) copy-start(s32[2,64,1,2]{1,3,2,0:T(2,128)} %param.7) | copy-start | bytes 3076
  2.9 29.4 %all-to-all-start = ((f32[64,4,128]{2,1,0:T(4,128)}), f32[64,4,128]{2,1,0:T(4,128)S(1)}, u32[]{:S(2)}, u32[]{:S(2)}) async-start(f32[64,4,128]{2,1,0:T(4,128)} %sent_rows.1), calls=%async_computation | async-start | bytes 262144 | tf_op jit(solution)/shard_map/all_to_all | solution.py:190
  22.2 1.2 %copy-start = (bf16[2,1,1792,128]{3,2,1,0:T(8,128)(2,1)S(1)}, bf16[2,1,1792,128]{3,2,1,0:T(8,128)(2,1)}, u32[]{:S(2)}) copy-start(bf16[2,1,1792,128]{3,2,1,0:T(8,128)(2,1)} %grads.3) | copy-start | bytes 2752516
  23.3 1.2 %copy-start.1 = (f32[1,1792,128]{2,1,0:T(8,128)S(1)}, f32[1,1792,128]{2,1,0:T(8,128)}, u32[]{:S(2)}) copy-start(f32[1,1792,128]{2,1,0:T(8,128)} %error.3) | copy-start | bytes 2752516
  24.5 7.9 %copy-start.2 = (f32[1792,128]{1,0:T(8,128)S(1)}, f32[1792,128]{1,0:T(8,128)}, u32[]{:S(2)}) copy-start(f32[1792,128]{1,0:T(8,128)} %accum.1) | copy-start | bytes 2752516

commit v4 on v3

--- a/solution.py
+++ b/solution.py
@@ -18,11 +18,14 @@
 H_ROWS = 16
 KIB = 1024
 ROOM = 12 * 1024 * KIB
-NEARLY_ALL = (63 * 1024 + 256) * KIB
 
 
 def kernel_params(limit=ROOM):
     return pltpu.CompilerParams(vmem_limit_bytes=limit)
+
+
+def in_hbm(array):
+    return pltpu.with_memory_space_constraint(array, pltpu.HBM)
 
 
 def send_kernel(picks, grads, error, rows, halves, wholes, half_sems, whole_sems):
@@ -73,7 +76,7 @@
 def sent_rows(picks, grads, error, copies):
     return pl.pallas_call(
         send_kernel,
-        out_shape=jax.ShapeDtypeStruct((copies, SENT, BLOCK), jnp.float32),
+        out_shape=pltpu.VMEM((copies, SENT, BLOCK), jnp.float32),
         in_specs=[
             pl.BlockSpec(memory_space=pltpu.SMEM),
             pl.BlockSpec(memory_space=pltpu.HBM),
@@ -86,7 +89,7 @@
             pltpu.SemaphoreType.DMA((SENT,)),
             pltpu.SemaphoreType.DMA((SENT,)),
         ],
-        compiler_params=kernel_params(NEARLY_ALL),
+        compiler_params=kernel_params(),
         name="sent_rows",
     )(picks, grads, error)
 
@@ -183,7 +186,8 @@
 
 
 def local(grads, error_in, accum_in, picks):
-    table = jnp.swapaxes(picks[:, :, 0, :], 1, 2)
+    table = in_hbm(jnp.swapaxes(picks[:, :, 0, :], 1, 2))
+    grads, error_in = in_hbm(grads), in_hbm(error_in)
     count = lax.axis_size("rep")
     members = exchange_order(count)
     rows = sent_rows(table, grads, error_in, count)

time: 34 us -> 34 us (level)
  local copies, waits for them, and re-layouts: 2.36 us -> 0.01 us
  Pallas kernels: 6.05 us -> 7.49 us
  waiting for transfers between devices: 5.38 us -> 6.3 us
    unnamed x8 -> x2, local copies, waits for them, and re-layouts: 2.36 us -> 0.01 us
    pallas_call x1, Pallas kernels: 2.47 us -> 3.92 us  [next_error(): pl.pallas_call(error_kernel, grid=(tiles,), out_shape=(jax.ShapeDtypeStru...]
    all_to_all x1, waiting for transfers between devices: 5.38 us -> 6.3 us  [local(): lax.all_to_all(rows, 'rep', 0, 0, axis_index_groups=[members], tiled=True)]
  transfers between devices with their start and end apart: 1 -> 1, of which waited for: 1 -> 1; matrix products, arithmetic and copies ran while one was open for 0% -> 0% of each run, Pallas kernels for 7% -> 12%
where the time goes in v4:
time: 34 us; the launch traced here: 33.7 us
  starting transfers between devices  19.2 us (56%)
  Pallas kernels  7.49 us (22%)
  waiting for transfers between devices  6.3 us (19%)
  between operations  0.65 us (2%)
    all_to_all x1, starting transfers between devices, local(): lax.all_to_all(rows, 'rep', 0, 0, axis_index_groups=[members], tiled=True)  19.2 us
    all_to_all x1, waiting for transfers between devices, local(): lax.all_to_all(rows, 'rep', 0, 0, axis_index_groups=[members], tiled=True)  6.3 us
    pallas_call x1, Pallas kernels, next_error(): pl.pallas_call(error_kernel, grid=(tiles,), out_shape=(jax.ShapeDtypeStru...  3.92 us
    pallas_call x1, Pallas kernels, sent_rows(): pl.pallas_call(send_kernel, out_shape=pltpu.VMEM((copies, SENT, BLOCK), j...  2.28 us
    pallas_call x1, Pallas kernels, add_rows(): pl.pallas_call(functools.partial(add_kernel, members), out_shape=jax.Shap...  1.29 us
  transfers between devices with their start and end apart: 1, of which 1 were waited for; matrix products, arithmetic and copies ran while one was open for 0% of the time, Pallas kernels for 12%

profile of v4, /device:TPU:24, one launch (start us, length us, event | category | flops | bytes accessed | tf_op | source)
XLA Modules:
  0.0 33.7 jit_solution(533681583029297080)
XLA Ops:
  0.6 2.3 %sent_rows.1 = f32[64,4,128]{2,1,0:T(4,128)} custom-call(s32[2,2,64]{2,1,0:T(2,128)} %bitcast.5, bf16[2,1,1792,128]{3,2,1,0:T(8,128)(2,1)} %grads.3, f32[1,1792,128]{2,1,0:T(8,128)} %error.3), custom_call_target="tpu_custom_call" | custom-call | tf_op jit(solution)/shard_map/sent_rows/pallas_call | solution.py:77
  2.9 19.2 %all-to-all-start = ((f32[64,4,128]{2,1,0:T(4,128)}), f32[64,4,128]{2,1,0:T(4,128)S(1)}, u32[]{:S(2)}, u32[]{:S(2)}) async-start(f32[64,4,128]{2,1,0:T(4,128)} %sent_rows.1), calls=%async_computation | async-start | bytes 262144 | tf_op jit(solution)/shard_map/all_to_all | solution.py:194
  22.1 0.0 copy-start
  22.1 3.9 %next_error.1 = (f32[1,1792,128]{2,1,0:T(8,128)}, bf16[1792,256]{1,0:T(8,128)(2,1)S(1)}) custom-call(s32[2,2,64]{2,1,0:T(2,128)} %bitcast.6, s32[2,2,64]{2,1,0:T(2,128)} %bitcast.7, bf16[2,1,1792,128]{3,2,1,0:T(8,128)(2,1)} %grads.3, f32[1,1792,128]{2,1,0:T(8,128)} %error.3), custom_call_target="tpu_custom_call" | custom-call | flops 1835008 | bytes 3670016 | tf_op jit(solution)/shard_map/next_error/pallas_call | solution.py:120
  26.1 6.3 %all-to-all-done = f32[64,4,128]{2,1,0:T(4,128)S(1)} async-done(((f32[64,4,128]{2,1,0:T(4,128)}), f32[64,4,128]{2,1,0:T(4,128)S(1)}, u32[]{:S(2)}, u32[]{:S(2)}) %all-to-all-start) | async-done | bytes 131104 | tf_op jit(solution)/shard_map/all_to_all | solution.py:194
  32.4 0.0 copy-done
  32.4 1.3 %add_rows.1 = f32[1792,128]{1,0:T(8,128)} custom-call(bf16[1792,256]{1,0:T(8,128)(2,1)S(1)} %get-tuple-element.4.hot, f32[256,128]{1,0:T(8,128)S(1)} %bitcast.4, f32[1792,128]{1,0:T(8,128)S(1)} %copy-done), custom_call_target="tpu_custom_call" | custom-call | tf_op jit(solution)/shard_map/add_rows/pallas_call | solution.py:168
Async XLA Ops:
  2.9 29.4 %all-to-all-start = ((f32[64,4,128]{2,1,0:T(4,128)}), f32[64,4,128]{2,1,0:T(4,128)S(1)}, u32[]{:S(2)}, u32[]{:S(2)}) async-start(f32[64,4,128]{2,1,0:T(4,128)} %sent_rows.1), calls=%async_computation | async-start | bytes 262144 | tf_op jit(solution)/shard_map/all_to_all | solution.py:194
  22.1 10.2 %copy-start = (f32[1792,128]{1,0:T(8,128)S(1)}, f32[1792,128]{1,0:T(8,128)}, u32[]{:S(2)}) copy-start(f32[1792,128]{1,0:T(8,128)} %accum.1) | copy-start | bytes 2752516

commit v5 on v4

v5 whole, which is shorter than its diff:
```python
import functools

import jax
import jax.numpy as jnp
from jax import lax
from jax.experimental import pallas as pl
from jax.experimental.pallas import tpu as pltpu
from jax.sharding import PartitionSpec as P

STEPS = 2
PICKS = 2
BLOCK = 128
SENT = STEPS * PICKS
WIDE = 4
FIRST_Z = 11
FIRST_X = 1
EARLY_Z = 5
F_ROWS = 8
H_ROWS = 16
KIB = 1024
ROOM = 16 * 1024 * KIB


def kernel_params(limit=ROOM):
    return pltpu.CompilerParams(vmem_limit_bytes=limit)


def in_hbm(array):
    return pltpu.with_memory_space_constraint(array, pltpu.HBM)


def starts_early(replica):
    return replica < EARLY_Z * WIDE


def tile_error(step_tiles, tile_in, own, first):
    index = lax.broadcasted_iota(jnp.int32, tile_in.shape, 0) + first
    left = tile_in
    for step in range(STEPS):
        left = step_tiles[step].astype(jnp.float32) + left
        for k in range(PICKS):
            sent = index == own[step * PICKS + k]
            left = jnp.where(sent, jnp.float32(0.0), left)
    return left


def one_hot(order, first, size):
    index = lax.broadcasted_iota(jnp.int32, (size, order.shape[1]), 0) + first
    hits = jnp.where(index == order, jnp.float32(1.0), jnp.float32(0.0))
    return hits.astype(jnp.bfloat16)


def row_of(tile, at):
    index = lax.broadcasted_iota(jnp.int32, tile.shape, 0)
    kept = jnp.where(index == at, tile, jnp.float32(0.0))
    return jnp.sum(kept, axis=0, keepdims=True)


def prepare_kernel(
    picks, table, grads, error, accum,
    rows, order, own, hot, held, error_out,
    halves, wholes, steps, errors, half_sems, whole_sems, held_sem, sems,
):
    replica = lax.axis_index("rep")
    chosen = [picks[j // PICKS, j % PICKS, replica] for j in range(SENT)]
    copies = []
    for j in range(SENT):
        base = pl.multiple_of((chosen[j] // F_ROWS) * F_ROWS, F_ROWS)
        copies.append(
            pltpu.make_async_copy(
                error.at[0, pl.ds(base, F_ROWS), :], wholes.at[j], whole_sems.at[j]
            )
        )
        base = pl.multiple_of((chosen[j] // H_ROWS) * H_ROWS, H_ROWS)
        part = pl.ds(0, j // PICKS + 1)
        copies.append(
            pltpu.make_async_copy(
                grads.at[part, 0, pl.ds(base, H_ROWS), :],
                halves.at[j, part],
                half_sems.at[j],
            )
        )
    for copy in copies:
        copy.start()
    order[...] = jnp.concatenate(
        [table[j // PICKS, pl.ds(j % PICKS, 1), :] for j in range(SENT)], axis=1
    )
    for j in range(SENT):
        own[pl.ds(j, 1), :] = jnp.full((1, BLOCK), chosen[j], jnp.int32)
    for copy in copies:
        copy.wait()

    sent = []
    for j in range(SENT):
        at = lax.rem(chosen[j], H_ROWS)
        value = row_of(halves[j, 0].astype(jnp.float32), at)
        value = value + row_of(wholes[j], lax.rem(chosen[j], F_ROWS))
        if j >= PICKS:
            again = (chosen[j] == chosen[0]) | (chosen[j] == chosen[1])
            value = jnp.where(again, jnp.float32(0.0), value)
            value = row_of(halves[j, 1].astype(jnp.float32), at) + value
        sent.append(value)
    block = jnp.concatenate(sent, axis=0)
    for peer in range(rows.shape[0]):
        rows[peer] = block

    tiles = sems.shape[1]
    size = errors.shape[0] // tiles

    @pl.when(starts_early(replica))
    def _():
        hold = pltpu.make_async_copy(accum, held, held_sem)
        loads, stores = [], []
        for tile in range(tiles):
            part = pl.ds(tile * size, size)
            loads.append((
                pltpu.make_async_copy(
                    grads.at[:, 0, part, :], steps.at[:, part, :], sems.at[0, tile]
                ),
                pltpu.make_async_copy(
                    error.at[0, part, :], errors.at[part, :], sems.at[1, tile]
                ),
            ))
            for load in loads[-1]:
                load.start()
        hold.start()
        for tile in range(tiles):
            part = pl.ds(tile * size, size)
            hot[part, :] = one_hot(order[...], tile * size, size)
            for load in loads[tile]:
                load.wait()
            pair = [steps[step, part, :] for step in range(STEPS)]
            errors[part, :] = tile_error(pair, errors[part, :], chosen, tile * size)
            stores.append(
                pltpu.make_async_copy(
                    errors.at[part, :], error_out.at[0, part, :], sems.at[2, tile]
                )
            )
            stores[-1].start()
        hold.wait()
        for store in stores:
            store.wait()


def prepare(picks, grads, error, accum, tiles=7):
    blocks = accum.shape[0]
    count = picks.shape[2]
    return pl.pallas_call(
        prepare_kernel,
        out_shape=(
            pltpu.VMEM((count, SENT, BLOCK), jnp.float32),
            pltpu.VMEM((1, SENT * count), jnp.int32),
            pltpu.VMEM((F_ROWS, BLOCK), jnp.int32),
            pltpu.VMEM((blocks, SENT * count), jnp.bfloat16),
            pltpu.VMEM(accum.shape, jnp.float32),
            pltpu.HBM(error.shape, jnp.float32),
        ),
        in_specs=[
            pl.BlockSpec(memory_space=pltpu.SMEM),
            pl.BlockSpec(memory_space=pltpu.VMEM),
        ]
        + [pl.BlockSpec(memory_space=pltpu.HBM)] * 3,
        out_specs=tuple(
            [pl.BlockSpec(memory_space=pltpu.VMEM)] * 5
            + [pl.BlockSpec(memory_space=pltpu.HBM)]
        ),
        scratch_shapes=[
            pltpu.VMEM((SENT, STEPS, H_ROWS, BLOCK), jnp.bfloat16),
            pltpu.VMEM((SENT, F_ROWS, BLOCK), jnp.float32),
            pltpu.VMEM((STEPS,) + accum.shape, jnp.bfloat16),
            pltpu.VMEM(accum.shape, jnp.float32),
            pltpu.SemaphoreType.DMA((SENT,)),
            pltpu.SemaphoreType.DMA((SENT,)),
            pltpu.SemaphoreType.DMA(()),
            pltpu.SemaphoreType.DMA((3, tiles)),
        ],
        compiler_params=kernel_params(),
        name="prepare",
    )(picks, picks, grads, error, accum)


def finish_kernel(
    members, order, own, hot, held, rows, grads, error, accum, _,
    error_out, accum_out, turned, steps, errors, sums, sems,
):
    replica = lax.axis_index("rep")
    tiles = sems.shape[1]
    size = sums.shape[0] // tiles
    count = len(members)
    for place, owner in enumerate(members):
        turned[pl.ds(owner, SENT, count), :] = rows[pl.ds(place * SENT, SENT), :]
    value = turned[...]
    high = value.astype(jnp.bfloat16)
    low = (value - high.astype(jnp.float32)).astype(jnp.bfloat16)
    pair = jnp.concatenate([high, low], axis=1)

    def store_sum(tile, hot_tile, base):
        part = pl.ds(tile * size, size)
        both = jnp.dot(hot_tile, pair, preferred_element_type=jnp.float32)
        sums[part, :] = base + (both[:, :BLOCK] + both[:, BLOCK:])
        copy = pltpu.make_async_copy(
            sums.at[part, :], accum_out.at[part, :], sems.at[0, tile]
        )
        copy.start()
        return copy

    early = starts_early(replica)

    @pl.when(early)
    def _():
        stores = []
        for tile in range(tiles):
            part = pl.ds(tile * size, size)
            stores.append(store_sum(tile, hot[part, :], held[part, :]))
        for store in stores:
            store.wait()

    @pl.when(jnp.logical_not(early))
    def _():
        loads, stores = [], []
        for tile in range(tiles):
            part = pl.ds(tile * size, size)
            loads.append((
                pltpu.make_async_copy(
                    accum.at[part, :], sums.at[part, :], sems.at[1, tile]
                ),
                pltpu.make_async_copy(
                    grads.at[:, 0, part, :], steps.at[:, part, :], sems.at[2, tile]
                ),
                pltpu.make_async_copy(
                    error.at[0, part, :], errors.at[part, :], sems.at[3, tile]
                ),
            ))
            for load in loads[-1]:
                load.start()
        mine = [own[pl.ds(j, 1), :] for j in range(SENT)]
        for tile in range(tiles):
            part = pl.ds(tile * size, size)
            hot_tile = one_hot(order[...], tile * size, size)
            for load in loads[tile]:
                load.wait()
            stores.append(store_sum(tile, hot_tile, sums[part, :]))
            step_tiles = [steps[step, part, :] for step in range(STEPS)]
            errors[part, :] = tile_error(step_tiles, errors[part, :], mine, tile * size)
            stores.append(
                pltpu.make_async_copy(
                    errors.at[part, :], error_out.at[0, part, :], sems.at[4, tile]
                )
            )
            stores[-1].start()
        for store in stores:
            store.wait()


def finish(members, order, own, hot, held, rows, grads, error, accum, done, tiles=7):
    return pl.pallas_call(
        functools.partial(finish_kernel, members),
        out_shape=(
            pltpu.HBM(error.shape, jnp.float32),
            pltpu.HBM(accum.shape, jnp.float32),
        ),
        in_specs=[pl.BlockSpec(memory_space=pltpu.VMEM)] * 5
        + [pl.BlockSpec(memory_space=pltpu.HBM)] * 4,
        out_specs=(
            pl.BlockSpec(memory_space=pltpu.HBM),
            pl.BlockSpec(memory_space=pltpu.HBM),
        ),
        input_output_aliases={8: 0},
        scratch_shapes=[
            pltpu.VMEM(rows.shape, jnp.float32),
            pltpu.VMEM((STEPS,) + accum.shape, jnp.bfloat16),
            pltpu.VMEM(accum.shape, jnp.float32),
            pltpu.VMEM(accum.shape, jnp.float32),
            pltpu.SemaphoreType.DMA((5, tiles)),
        ],
        compiler_params=kernel_params(),
        name="finish",
    )(order, own, hot, held, rows, grads, error, accum, done)


def exchange_order(count):
    first = FIRST_Z * WIDE + FIRST_X
    return [(first + place) % count for place in range(count)]


def local(grads, error_in, accum_in, picks):
    table = in_hbm(jnp.swapaxes(picks[:, :, 0, :], 1, 2))
    grads, error_in, accum_in = in_hbm(grads), in_hbm(error_in), in_hbm(accum_in)
    count = lax.axis_size("rep")
    members = exchange_order(count)
    rows, order, own, hot, held, done = prepare(table, grads, error_in, accum_in)
    rows = lax.all_to_all(
        rows, "rep", 0, 0, axis_index_groups=[members], tiled=True
    )
    rows = rows.reshape(count * SENT, BLOCK)
    error, accum = finish(
        members, order, own, hot, held, rows, grads, error_in, accum_in, in_hbm(done)
    )
    return (accum, error)


def solution(mesh):
    placed = (
        P(None, "rep", "tp", None),
        P("rep", "tp", None),
        P("tp", None),
        P(None, None, "tp", None),
    )
    return jax.shard_map(
        local,
        mesh=mesh,
        in_specs=placed,
        out_specs=(P("tp", None), P("rep", "tp", None)),
        check_vma=False,
    )
```

time: 34 us -> 33.5 us (0.985)
  blocking collectives: 0 us -> 27 us
  starting transfers between devices: 19.2 us -> 0 us
  waiting for transfers between devices: 6.3 us -> 0 us
  Pallas kernels: 7.49 us -> 5.67 us
    all_to_all x0 -> x1, blocking collectives: none -> 27 us  [local(): lax.all_to_all(rows, 'rep', 0, 0, axis_index_groups=[members], tiled=True)]
    all_to_all x1 -> x0, starting transfers between devices: 19.2 us -> none  [local(): lax.all_to_all(rows, 'rep', 0, 0, axis_index_groups=[members], tiled=True)]
    all_to_all x1 -> x0, waiting for transfers between devices: 6.3 us -> none  [local(): lax.all_to_all(rows, 'rep', 0, 0, axis_index_groups=[members], tiled=True)]
    pallas_call x3 -> x2, Pallas kernels: 7.49 us -> 5.67 us  [the longest x1 4.11 us: prepare(): pl.pallas_call(prepare_kernel, out_shape=(pltpu.VMEM((count, SENT, BLOCK)...]
  transfers between devices with their start and end apart: 1 -> 0, of which waited for: 1 -> 0; matrix products, arithmetic and copies ran while one was open for 0% -> 0% of each run, Pallas kernels for 12% -> 0%
where the time goes in v5:
time: 33.5 us; the launch traced here: 33.3 us
  blocking collectives  27 us (81%)
  Pallas kernels  5.67 us (17%)
  between operations  0.64 us (2%)
    all_to_all x1, blocking collectives, local(): lax.all_to_all(rows, 'rep', 0, 0, axis_index_groups=[members], tiled=True)  27 us
    pallas_call x1, Pallas kernels, prepare(): pl.pallas_call(prepare_kernel, out_shape=(pltpu.VMEM((count, SENT, BLOCK)...  4.11 us
    pallas_call x1, Pallas kernels, finish(): pl.pallas_call(functools.partial(finish_kernel, members), out_shape=(pltp...  1.55 us

profile of v5, /device:TPU:24, one launch (start us, length us, event | category | flops | bytes accessed | tf_op | source)
XLA Modules:
  0.0 33.3 jit_solution(16609027431722059448)
XLA Ops:
  0.6 4.1 %prepare.1 = (f32[64,4,128]{2,1,0:T(4,128)S(1)}, s32[1,256]{1,0:T(1,128)S(1)}, s32[8,128]{1,0:T(8,128)S(1)}, bf16[1792,256]{1,0:T(8,128)(2,1)S(1)}, f32[1792,128]{1,0:T(8,128)S(1)}, /*index=5*/f32[1,1792,128]{2,1,0:T(8,128)}) custom-call(s32[2,2,64]{2,1,0:T(2,128)} %bitcast.5, s32[2,2,64]{2,1,0:T(2,128)} %bitcast.6, bf16[2,1,1792,128]{3,2,1,0:T(8,128)(2,1)} %grads.3, ...), custom_call_target="tpu_custom_call" | custom-call | tf_op jit(solution)/shard_map/prepare/pallas_call | solution.py:148
  4.7 27.0 %all_to_all.5 = f32[64,4,128]{2,1,0:T(4,128)S(1)} all-to-all(f32[64,4,128]{2,1,0:T(4,128)S(1)} %get-tuple-element.14), channel_id=1, replica_groups={{360,368,376,384,392,400,408,416,424,432,440,448,456,464,472,480,488,49..., dimensions={0} | all-to-all | bytes 262144 | tf_op jit(solution)/shard_map/all_to_all | solution.py:292
  31.7 1.6 %finish.1 = (f32[1,1792,128]{2,1,0:T(8,128)}, f32[1792,128]{1,0:T(8,128)}) custom-call(s32[1,256]{1,0:T(1,128)S(1)} %get-tuple-element.10.order, s32[8,128]{1,0:T(8,128)S(1)} %get-tuple-element.11.own, bf16[1792,256]{1,0:T(8,128)(2,1)S(1)} %get-tuple-element.12.hot, f32[1792,128]{1,0:T(8,128)S(1)} %get-tuple-element.13.held, ...), custom_call_target="tpu_custom_call", output_to_operand_aliasing={{0}: (8, {})} | custom-call | tf_op jit(solution)/shard_map/finish/pallas_call | solution.py:256

commit v6 on v5

--- a/solution.py
+++ b/solution.py
@@ -59,9 +59,11 @@
 def prepare_kernel(
     picks, table, grads, error, accum,
     rows, order, own, hot, held, error_out,
-    halves, wholes, steps, errors, half_sems, whole_sems, held_sem, sems,
+    lanes, halves, wholes, steps, errors, half_sems, whole_sems, one_sems, sems,
 ):
     replica = lax.axis_index("rep")
+    look = pltpu.make_async_copy(table, lanes, one_sems.at[0])
+    look.start()
     chosen = [picks[j // PICKS, j % PICKS, replica] for j in range(SENT)]
     copies = []
     for j in range(SENT):
@@ -82,8 +84,9 @@
         )
     for copy in copies:
         copy.start()
+    look.wait()
     order[...] = jnp.concatenate(
-        [table[j // PICKS, pl.ds(j % PICKS, 1), :] for j in range(SENT)], axis=1
+        [lanes[j // PICKS, pl.ds(j % PICKS, 1), :] for j in range(SENT)], axis=1
     )
     for j in range(SENT):
         own[pl.ds(j, 1), :] = jnp.full((1, BLOCK), chosen[j], jnp.int32)
@@ -109,7 +112,7 @@
 
     @pl.when(starts_early(replica))
     def _():
-        hold = pltpu.make_async_copy(accum, held, held_sem)
+        hold = pltpu.make_async_copy(accum, held, one_sems.at[1])
         loads, stores = [], []
         for tile in range(tiles):
             part = pl.ds(tile * size, size)
@@ -155,23 +158,21 @@
             pltpu.VMEM(accum.shape, jnp.float32),
             pltpu.HBM(error.shape, jnp.float32),
         ),
-        in_specs=[
-            pl.BlockSpec(memory_space=pltpu.SMEM),
-            pl.BlockSpec(memory_space=pltpu.VMEM),
-        ]
-        + [pl.BlockSpec(memory_space=pltpu.HBM)] * 3,
+        in_specs=[pl.BlockSpec(memory_space=pltpu.SMEM)]
+        + [pl.BlockSpec(memory_space=pltpu.HBM)] * 4,
         out_specs=tuple(
             [pl.BlockSpec(memory_space=pltpu.VMEM)] * 5
             + [pl.BlockSpec(memory_space=pltpu.HBM)]
         ),
         scratch_shapes=[
+            pltpu.VMEM(picks.shape, jnp.int32),
             pltpu.VMEM((SENT, STEPS, H_ROWS, BLOCK), jnp.bfloat16),
             pltpu.VMEM((SENT, F_ROWS, BLOCK), jnp.float32),
             pltpu.VMEM((STEPS,) + accum.shape, jnp.bfloat16),
             pltpu.VMEM(accum.shape, jnp.float32),
             pltpu.SemaphoreType.DMA((SENT,)),
             pltpu.SemaphoreType.DMA((SENT,)),
-            pltpu.SemaphoreType.DMA(()),
+            pltpu.SemaphoreType.DMA((2,)),
             pltpu.SemaphoreType.DMA((3, tiles)),
         ],
         compiler_params=kernel_params(),
@@ -187,14 +188,16 @@
     tiles = sems.shape[1]
     size = sums.shape[0] // tiles
     count = len(members)
-    for place, owner in enumerate(members):
-        turned[pl.ds(owner, SENT, count), :] = rows[pl.ds(place * SENT, SENT), :]
-    value = turned[...]
-    high = value.astype(jnp.bfloat16)
-    low = (value - high.astype(jnp.float32)).astype(jnp.bfloat16)
-    pair = jnp.concatenate([high, low], axis=1)
-
-    def store_sum(tile, hot_tile, base):
+
+    def split_rows():
+        for place, owner in enumerate(members):
+            turned[pl.ds(owner, SENT, count), :] = rows[pl.ds(place * SENT, SENT), :]
+        value = turned[...]
+        high = value.astype(jnp.bfloat16)
+        low = (value - high.astype(jnp.float32)).astype(jnp.bfloat16)
+        return jnp.concatenate([high, low], axis=1)
+
+    def store_sum(tile, hot_tile, pair, base):
         part = pl.ds(tile * size, size)
         both = jnp.dot(hot_tile, pair, preferred_element_type=jnp.float32)
         sums[part, :] = base + (both[:, :BLOCK] + both[:, BLOCK:])
@@ -208,10 +211,11 @@
 
     @pl.when(early)
     def _():
+        pair = split_rows()
         stores = []
         for tile in range(tiles):
             part = pl.ds(tile * size, size)
-            stores.append(store_sum(tile, hot[part, :], held[part, :]))
+            stores.append(store_sum(tile, hot[part, :], pair, held[part, :]))
         for store in stores:
             store.wait()
 
@@ -233,13 +237,14 @@
             ))
             for load in loads[-1]:
                 load.start()
+        pair = split_rows()
         mine = [own[pl.ds(j, 1), :] for j in range(SENT)]
         for tile in range(tiles):
             part = pl.ds(tile * size, size)
             hot_tile = one_hot(order[...], tile * size, size)
             for load in loads[tile]:
                 load.wait()
-            stores.append(store_sum(tile, hot_tile, sums[part, :]))
+            stores.append(store_sum(tile, hot_tile, pair, sums[part, :]))
             step_tiles = [steps[step, part, :] for step in range(STEPS)]
             errors[part, :] = tile_error(step_tiles, errors[part, :], mine, tile * size)
             stores.append(

time: 33.5 us -> 33.5 us (level)
  no operation moved by 1% of the time
where the time goes in v6:
time: 33.5 us; the launch traced here: 33.3 us
  blocking collectives  27 us (81%)
  Pallas kernels  5.63 us (17%)
  between operations  0.64 us (2%)
    all_to_all x1, blocking collectives, local(): lax.all_to_all(rows, 'rep', 0, 0, axis_index_groups=[members], tiled=True)  27 us
    pallas_call x1, Pallas kernels, prepare(): pl.pallas_call(prepare_kernel, out_shape=(pltpu.VMEM((count, SENT, BLOCK)...  4.09 us
    pallas_call x1, Pallas kernels, finish(): pl.pallas_call(functools.partial(finish_kernel, members), out_shape=(pltp...  1.54 us

profile of v6, /device:TPU:24, one launch (start us, length us, event | category | flops | bytes accessed | tf_op | source)
XLA Modules:
  0.0 33.3 jit_solution(218346855569302566)
XLA Ops:
  0.6 4.1 %prepare.1 = (f32[64,4,128]{2,1,0:T(4,128)S(1)}, s32[1,256]{1,0:T(1,128)S(1)}, s32[8,128]{1,0:T(8,128)S(1)}, bf16[1792,256]{1,0:T(8,128)(2,1)S(1)}, f32[1792,128]{1,0:T(8,128)S(1)}, /*index=5*/f32[1,1792,128]{2,1,0:T(8,128)}) custom-call(s32[2,2,64]{2,1,0:T(2,128)} %bitcast.5, s32[2,2,64]{2,1,0:T(2,128)} %bitcast.6, bf16[2,1,1792,128]{3,2,1,0:T(8,128)(2,1)} %grads.3, ...), custom_call_target="tpu_custom_call" | custom-call | tf_op jit(solution)/shard_map/prepare/pallas_call | solution.py:151
  4.7 27.0 %all_to_all.5 = f32[64,4,128]{2,1,0:T(4,128)S(1)} all-to-all(f32[64,4,128]{2,1,0:T(4,128)S(1)} %get-tuple-element.14), channel_id=1, replica_groups={{360,368,376,384,392,400,408,416,424,432,440,448,456,464,472,480,488,49..., dimensions={0} | all-to-all | bytes 262144 | tf_op jit(solution)/shard_map/all_to_all | solution.py:297
  31.7 1.5 %finish.1 = (f32[1,1792,128]{2,1,0:T(8,128)}, f32[1792,128]{1,0:T(8,128)}) custom-call(s32[1,256]{1,0:T(1,128)S(1)} %get-tuple-element.10.order, s32[8,128]{1,0:T(8,128)S(1)} %get-tuple-element.11.own, bf16[1792,256]{1,0:T(8,128)(2,1)S(1)} %get-tuple-element.12.hot, f32[1792,128]{1,0:T(8,128)S(1)} %get-tuple-element.13.held, ...), custom_call_target="tpu_custom_call", output_to_operand_aliasing={{0}: (8, {})} | custom-call | tf_op jit(solution)/shard_map/finish/pallas_call | solution.py:261

commit v7 on v6

--- a/solution.py
+++ b/solution.py
@@ -57,86 +57,73 @@
 
 
 def prepare_kernel(
-    picks, table, grads, error, accum,
+    picks, grads, error, accum,
     rows, order, own, hot, held, error_out,
-    lanes, halves, wholes, steps, errors, half_sems, whole_sems, one_sems, sems,
+    spots, lanes, steps, errors, one_sems, load_sems, store_sems,
 ):
     replica = lax.axis_index("rep")
-    look = pltpu.make_async_copy(table, lanes, one_sems.at[0])
+    look = pltpu.make_async_copy(picks, spots, one_sems.at[0])
     look.start()
-    chosen = [picks[j // PICKS, j % PICKS, replica] for j in range(SENT)]
-    copies = []
-    for j in range(SENT):
-        base = pl.multiple_of((chosen[j] // F_ROWS) * F_ROWS, F_ROWS)
-        copies.append(
+    loads = []
+    chunks = load_sems.shape[1]
+    size = errors.shape[0] // chunks
+    for chunk in range(chunks):
+        part = pl.ds(chunk * size, size)
+        loads.append(
             pltpu.make_async_copy(
-                error.at[0, pl.ds(base, F_ROWS), :], wholes.at[j], whole_sems.at[j]
+                error.at[0, part, :], errors.at[part, :], load_sems.at[0, chunk]
             )
         )
-        base = pl.multiple_of((chosen[j] // H_ROWS) * H_ROWS, H_ROWS)
-        part = pl.ds(0, j // PICKS + 1)
-        copies.append(
+        loads.append(
             pltpu.make_async_copy(
-                grads.at[part, 0, pl.ds(base, H_ROWS), :],
-                halves.at[j, part],
-                half_sems.at[j],
+                grads.at[:, 0, part, :], steps.at[:, part, :], load_sems.at[1, chunk]
             )
         )
-    for copy in copies:
-        copy.start()
+    for load in loads:
+        load.start()
+    scan = pltpu.make_async_copy(picks, lanes, one_sems.at[1])
+    scan.start()
     look.wait()
+    chosen = [spots[j // PICKS, j % PICKS, replica] for j in range(SENT)]
+    for j in range(SENT):
+        own[pl.ds(j, 1), :] = jnp.full((1, BLOCK), chosen[j], jnp.int32)
+    scan.wait()
     order[...] = jnp.concatenate(
         [lanes[j // PICKS, pl.ds(j % PICKS, 1), :] for j in range(SENT)], axis=1
     )
-    for j in range(SENT):
-        own[pl.ds(j, 1), :] = jnp.full((1, BLOCK), chosen[j], jnp.int32)
-    for copy in copies:
-        copy.wait()
+    for load in loads:
+        load.wait()
 
     sent = []
     for j in range(SENT):
-        at = lax.rem(chosen[j], H_ROWS)
-        value = row_of(halves[j, 0].astype(jnp.float32), at)
-        value = value + row_of(wholes[j], lax.rem(chosen[j], F_ROWS))
+        base = pl.multiple_of((chosen[j] // H_ROWS) * H_ROWS, H_ROWS)
+        at = chosen[j] - base
+        near = pl.ds(base, H_ROWS)
+        value = steps[0, near, :].astype(jnp.float32) + errors[near, :]
         if j >= PICKS:
             again = (chosen[j] == chosen[0]) | (chosen[j] == chosen[1])
             value = jnp.where(again, jnp.float32(0.0), value)
-            value = row_of(halves[j, 1].astype(jnp.float32), at) + value
-        sent.append(value)
+            value = steps[1, near, :].astype(jnp.float32) + value
+        sent.append(row_of(value, at))
     block = jnp.concatenate(sent, axis=0)
     for peer in range(rows.shape[0]):
         rows[peer] = block
 
-    tiles = sems.shape[1]
-    size = errors.shape[0] // tiles
-
     @pl.when(starts_early(replica))
     def _():
-        hold = pltpu.make_async_copy(accum, held, one_sems.at[1])
-        loads, stores = [], []
-        for tile in range(tiles):
-            part = pl.ds(tile * size, size)
-            loads.append((
-                pltpu.make_async_copy(
-                    grads.at[:, 0, part, :], steps.at[:, part, :], sems.at[0, tile]
-                ),
-                pltpu.make_async_copy(
-                    error.at[0, part, :], errors.at[part, :], sems.at[1, tile]
-                ),
-            ))
-            for load in loads[-1]:
-                load.start()
+        hold = pltpu.make_async_copy(accum, held, one_sems.at[2])
         hold.start()
+        tiles = store_sems.shape[0]
+        size = errors.shape[0] // tiles
+        stores = []
         for tile in range(tiles):
             part = pl.ds(tile * size, size)
             hot[part, :] = one_hot(order[...], tile * size, size)
-            for load in loads[tile]:
-                load.wait()
             pair = [steps[step, part, :] for step in range(STEPS)]
             errors[part, :] = tile_error(pair, errors[part, :], chosen, tile * size)
             stores.append(
                 pltpu.make_async_copy(
-                    errors.at[part, :], error_out.at[0, part, :], sems.at[2, tile]
+                    errors.at[part, :], error_out.at[0, part, :], store_sems.at[tile]
                 )
             )
             stores[-1].start()
@@ -145,7 +132,7 @@
             store.wait()
 
 
-def prepare(picks, grads, error, accum, tiles=7):
+def prepare(picks, grads, error, accum, chunks=4, tiles=7):
     blocks = accum.shape[0]
     count = picks.shape[2]
     return pl.pallas_call(
@@ -158,26 +145,23 @@
             pltpu.VMEM(accum.shape, jnp.float32),
             pltpu.HBM(error.shape, jnp.float32),
         ),
-        in_specs=[pl.BlockSpec(memory_space=pltpu.SMEM)]
-        + [pl.BlockSpec(memory_space=pltpu.HBM)] * 4,
+        in_specs=[pl.BlockSpec(memory_space=pltpu.HBM)] * 4,
         out_specs=tuple(
             [pl.BlockSpec(memory_space=pltpu.VMEM)] * 5
             + [pl.BlockSpec(memory_space=pltpu.HBM)]
         ),
         scratch_shapes=[
+            pltpu.SMEM(picks.shape, jnp.int32),
             pltpu.VMEM(picks.shape, jnp.int32),
-            pltpu.VMEM((SENT, STEPS, H_ROWS, BLOCK), jnp.bfloat16),
-            pltpu.VMEM((SENT, F_ROWS, BLOCK), jnp.float32),
             pltpu.VMEM((STEPS,) + accum.shape, jnp.bfloat16),
             pltpu.VMEM(accum.shape, jnp.float32),
-            pltpu.SemaphoreType.DMA((SENT,)),
-            pltpu.SemaphoreType.DMA((SENT,)),
-            pltpu.SemaphoreType.DMA((2,)),
-            pltpu.SemaphoreType.DMA((3, tiles)),
+            pltpu.SemaphoreType.DMA((3,)),
+            pltpu.SemaphoreType.DMA((2, chunks)),
+            pltpu.SemaphoreType.DMA((tiles,)),
         ],
         compiler_params=kernel_params(),
         name="prepare",
-    )(picks, picks, grads, error, accum)
+    )(picks, grads, error, accum)
 
 
 def finish_kernel(

time: 33.5 us -> 33.4 us (level)
  Pallas kernels: 5.63 us -> 4.83 us
  blocking collectives: 27 us -> 27.7 us
    pallas_call x1, Pallas kernels: 4.09 us -> 3.29 us  [prepare(): pl.pallas_call(prepare_kernel, out_shape=(pltpu.VMEM((count, SENT, BLOCK)...]
    all_to_all x1, blocking collectives: 27 us -> 27.7 us  [local(): lax.all_to_all(rows, 'rep', 0, 0, axis_index_groups=[members], tiled=True)]
where the time goes in v7:
time: 33.4 us; the launch traced here: 33.2 us
  blocking collectives  27.7 us (83%)
  Pallas kernels  4.83 us (14%)
  between operations  0.64 us (2%)
    all_to_all x1, blocking collectives, local(): lax.all_to_all(rows, 'rep', 0, 0, axis_index_groups=[members], tiled=True)  27.7 us
    pallas_call x1, Pallas kernels, prepare(): pl.pallas_call(prepare_kernel, out_shape=(pltpu.VMEM((count, SENT, BLOCK)...  3.29 us
    pallas_call x1, Pallas kernels, finish(): pl.pallas_call(functools.partial(finish_kernel, members), out_shape=(pltp...  1.54 us

profile of v7, /device:TPU:24, one launch (start us, length us, event | category | flops | bytes accessed | tf_op | source)
XLA Modules:
  0.0 33.2 jit_solution(12578777214699420054)
XLA Ops:
  0.6 3.3 %prepare.1 = (f32[64,4,128]{2,1,0:T(4,128)S(1)}, s32[1,256]{1,0:T(1,128)S(1)}, s32[8,128]{1,0:T(8,128)S(1)}, bf16[1792,256]{1,0:T(8,128)(2,1)S(1)}, f32[1792,128]{1,0:T(8,128)S(1)}, /*index=5*/f32[1,1792,128]{2,1,0:T(8,128)}) custom-call(s32[2,2,64]{2,1,0:T(2,128)} %bitcast.5, bf16[2,1,1792,128]{3,2,1,0:T(8,128)(2,1)} %grads.3, f32[1,1792,128]{2,1,0:T(8,128)} %error.3, ...), custom_call_target="tpu_custom_call" | custom-call | tf_op jit(solution)/shard_map/prepare/pallas_call | solution.py:138
  3.9 27.7 %all_to_all.5 = f32[64,4,128]{2,1,0:T(4,128)S(1)} all-to-all(f32[64,4,128]{2,1,0:T(4,128)S(1)} %get-tuple-element.14), channel_id=1, replica_groups={{360,368,376,384,392,400,408,416,424,432,440,448,456,464,472,480,488,49..., dimensions={0} | all-to-all | bytes 262144 | tf_op jit(solution)/shard_map/all_to_all | solution.py:281
  31.6 1.5 %finish.1 = (f32[1,1792,128]{2,1,0:T(8,128)}, f32[1792,128]{1,0:T(8,128)}) custom-call(s32[1,256]{1,0:T(1,128)S(1)} %get-tuple-element.10.order, s32[8,128]{1,0:T(8,128)S(1)} %get-tuple-element.11.own, bf16[1792,256]{1,0:T(8,128)(2,1)S(1)} %get-tuple-element.12.hot, f32[1792,128]{1,0:T(8,128)S(1)} %get-tuple-element.13.held, ...), custom_call_target="tpu_custom_call", output_to_operand_aliasing={{0}: (8, {})} | custom-call | tf_op jit(solution)/shard_map/finish/pallas_call | solution.py:245

commit v8 on v7

--- a/solution.py
+++ b/solution.py
@@ -12,9 +12,10 @@
 BLOCK = 128
 SENT = STEPS * PICKS
 WIDE = 4
-FIRST_Z = 11
-FIRST_X = 1
+FIRST_Z = 10
+FIRST_X = 2
 EARLY_Z = 5
+EARLY_TILES = (256, 512, 512, 256, 128, 128)
 F_ROWS = 8
 H_ROWS = 16
 KIB = 1024
@@ -181,8 +182,7 @@
         low = (value - high.astype(jnp.float32)).astype(jnp.bfloat16)
         return jnp.concatenate([high, low], axis=1)
 
-    def store_sum(tile, hot_tile, pair, base):
-        part = pl.ds(tile * size, size)
+    def store_sum(tile, part, hot_tile, pair, base):
         both = jnp.dot(hot_tile, pair, preferred_element_type=jnp.float32)
         sums[part, :] = base + (both[:, :BLOCK] + both[:, BLOCK:])
         copy = pltpu.make_async_copy(
@@ -197,9 +197,11 @@
     def _():
         pair = split_rows()
         stores = []
-        for tile in range(tiles):
-            part = pl.ds(tile * size, size)
-            stores.append(store_sum(tile, hot[part, :], pair, held[part, :]))
+        first = 0
+        for tile, size in enumerate(EARLY_TILES):
+            part = pl.ds(first, size)
+            first += size
+            stores.append(store_sum(tile, part, hot[part, :], pair, held[part, :]))
         for store in stores:
             store.wait()
 
@@ -228,7 +230,7 @@
             hot_tile = one_hot(order[...], tile * size, size)
             for load in loads[tile]:
                 load.wait()
-            stores.append(store_sum(tile, hot_tile, pair, sums[part, :]))
+            stores.append(store_sum(tile, part, hot_tile, pair, sums[part, :]))
             step_tiles = [steps[step, part, :] for step in range(STEPS)]
             errors[part, :] = tile_error(step_tiles, errors[part, :], mine, tile * size)
             stores.append(

time: 33.4 us -> 32.6 us (0.976)
  blocking collectives: 27.7 us -> 26.9 us
    all_to_all x1, blocking collectives: 27.7 us -> 26.9 us  [local(): lax.all_to_all(rows, 'rep', 0, 0, axis_index_groups=[members], tiled=True)]
where the time goes in v8:
time: 32.6 us; the launch traced here: 32.3 us
  blocking collectives  26.9 us (83%)
  Pallas kernels  4.85 us (15%)
  between operations  0.64 us (2%)
    all_to_all x1, blocking collectives, local(): lax.all_to_all(rows, 'rep', 0, 0, axis_index_groups=[members], tiled=True)  26.9 us
    pallas_call x1, Pallas kernels, prepare(): pl.pallas_call(prepare_kernel, out_shape=(pltpu.VMEM((count, SENT, BLOCK)...  3.29 us
    pallas_call x1, Pallas kernels, finish(): pl.pallas_call(functools.partial(finish_kernel, members), out_shape=(pltp...  1.56 us

profile of v8, /device:TPU:24, one launch (start us, length us, event | category | flops | bytes accessed | tf_op | source)
XLA Modules:
  0.0 32.3 jit_solution(18022196531770232873)
XLA Ops:
  0.6 3.3 %prepare.1 = (f32[64,4,128]{2,1,0:T(4,128)S(1)}, s32[1,256]{1,0:T(1,128)S(1)}, s32[8,128]{1,0:T(8,128)S(1)}, bf16[1792,256]{1,0:T(8,128)(2,1)S(1)}, f32[1792,128]{1,0:T(8,128)S(1)}, /*index=5*/f32[1,1792,128]{2,1,0:T(8,128)}) custom-call(s32[2,2,64]{2,1,0:T(2,128)} %bitcast.5, bf16[2,1,1792,128]{3,2,1,0:T(8,128)(2,1)} %grads.3, f32[1,1792,128]{2,1,0:T(8,128)} %error.3, ...), custom_call_target="tpu_custom_call" | custom-call | tf_op jit(solution)/shard_map/prepare/pallas_call | solution.py:139
  3.9 26.9 %all_to_all.5 = f32[64,4,128]{2,1,0:T(4,128)S(1)} all-to-all(f32[64,4,128]{2,1,0:T(4,128)S(1)} %get-tuple-element.14), channel_id=1, replica_groups={{336,344,352,360,368,376,384,392,400,408,416,424,432,440,448,456,464,47..., dimensions={0} | all-to-all | bytes 262144 | tf_op jit(solution)/shard_map/all_to_all | solution.py:283
  30.8 1.6 %finish.1 = (f32[1,1792,128]{2,1,0:T(8,128)}, f32[1792,128]{1,0:T(8,128)}) custom-call(s32[1,256]{1,0:T(1,128)S(1)} %get-tuple-element.10.order, s32[8,128]{1,0:T(8,128)S(1)} %get-tuple-element.11.own, bf16[1792,256]{1,0:T(8,128)(2,1)S(1)} %get-tuple-element.12.hot, f32[1792,128]{1,0:T(8,128)S(1)} %get-tuple-element.13.held, ...), custom_call_target="tpu_custom_call", output_to_operand_aliasing={{0}: (8, {})} | custom-call | tf_op jit(solution)/shard_map/finish/pallas_call | solution.py:247

commit v9 on v8

--- a/solution.py
+++ b/solution.py
@@ -12,10 +12,10 @@
 BLOCK = 128
 SENT = STEPS * PICKS
 WIDE = 4
-FIRST_Z = 10
+FIRST_Z = 11
 FIRST_X = 2
 EARLY_Z = 5
-EARLY_TILES = (256, 512, 512, 256, 128, 128)
+EARLY_TILES = (256,) * 7
 F_ROWS = 8
 H_ROWS = 16
 KIB = 1024

time: 32.6 us -> 32.4 us (level)
  no operation moved by 1% of the time
where the time goes in v9:
time: 32.4 us; the launch traced here: 32.1 us
  blocking collectives  26.7 us (82%)
  Pallas kernels  4.83 us (15%)
  between operations  0.64 us (2%)
    all_to_all x1, blocking collectives, local(): lax.all_to_all(rows, 'rep', 0, 0, axis_index_groups=[members], tiled=True)  26.7 us
    pallas_call x1, Pallas kernels, prepare(): pl.pallas_call(prepare_kernel, out_shape=(pltpu.VMEM((count, SENT, BLOCK)...  3.29 us
    pallas_call x1, Pallas kernels, finish(): pl.pallas_call(functools.partial(finish_kernel, members), out_shape=(pltp...  1.54 us

profile of v9, /device:TPU:24, one launch (start us, length us, event | category | flops | bytes accessed | tf_op | source)
XLA Modules:
  0.0 32.1 jit_solution(801719205157538168)
XLA Ops:
  0.6 3.3 %prepare.1 = (f32[64,4,128]{2,1,0:T(4,128)S(1)}, s32[1,256]{1,0:T(1,128)S(1)}, s32[8,128]{1,0:T(8,128)S(1)}, bf16[1792,256]{1,0:T(8,128)(2,1)S(1)}, f32[1792,128]{1,0:T(8,128)S(1)}, /*index=5*/f32[1,1792,128]{2,1,0:T(8,128)}) custom-call(s32[2,2,64]{2,1,0:T(2,128)} %bitcast.5, bf16[2,1,1792,128]{3,2,1,0:T(8,128)(2,1)} %grads.3, f32[1,1792,128]{2,1,0:T(8,128)} %error.3, ...), custom_call_target="tpu_custom_call" | custom-call | tf_op jit(solution)/shard_map/prepare/pallas_call | solution.py:139
  3.9 26.7 %all_to_all.5 = f32[64,4,128]{2,1,0:T(4,128)S(1)} all-to-all(f32[64,4,128]{2,1,0:T(4,128)S(1)} %get-tuple-element.14), channel_id=1, replica_groups={{368,376,384,392,400,408,416,424,432,440,448,456,464,472,480,488,496,50..., dimensions={0} | all-to-all | bytes 262144 | tf_op jit(solution)/shard_map/all_to_all | solution.py:283
  30.6 1.5 %finish.1 = (f32[1,1792,128]{2,1,0:T(8,128)}, f32[1792,128]{1,0:T(8,128)}) custom-call(s32[1,256]{1,0:T(1,128)S(1)} %get-tuple-element.10.order, s32[8,128]{1,0:T(8,128)S(1)} %get-tuple-element.11.own, bf16[1792,256]{1,0:T(8,128)(2,1)S(1)} %get-tuple-element.12.hot, f32[1792,128]{1,0:T(8,128)S(1)} %get-tuple-element.13.held, ...), custom_call_target="tpu_custom_call", output_to_operand_aliasing={{0}: (8, {})} | custom-call | tf_op jit(solution)/shard_map/finish/pallas_call | solution.py:247

commit v10 on v9

--- a/solution.py
+++ b/solution.py
@@ -12,7 +12,7 @@
 BLOCK = 128
 SENT = STEPS * PICKS
 WIDE = 4
-FIRST_Z = 11
+FIRST_Z = 12
 FIRST_X = 2
 EARLY_Z = 5
 EARLY_TILES = (256,) * 7

time: 32.4 us -> 33.8 us (1.043)
  blocking collectives: 26.7 us -> 28.1 us
    all_to_all x1, blocking collectives: 26.7 us -> 28.1 us  [local(): lax.all_to_all(rows, 'rep', 0, 0, axis_index_groups=[members], tiled=True)]
where the time goes in v10:
time: 33.8 us; the launch traced here: 33.6 us
  blocking collectives  28.1 us (83%)
  Pallas kernels  4.83 us (14%)
  between operations  0.64 us (2%)
    all_to_all x1, blocking collectives, local(): lax.all_to_all(rows, 'rep', 0, 0, axis_index_groups=[members], tiled=True)  28.1 us
    pallas_call x1, Pallas kernels, prepare(): pl.pallas_call(prepare_kernel, out_shape=(pltpu.VMEM((count, SENT, BLOCK)...  3.29 us
    pallas_call x1, Pallas kernels, finish(): pl.pallas_call(functools.partial(finish_kernel, members), out_shape=(pltp...  1.54 us

profile of v10, /device:TPU:24, one launch (start us, length us, event | category | flops | bytes accessed | tf_op | source)
XLA Modules:
  0.0 33.6 jit_solution(12815658715061583039)
XLA Ops:
  0.6 3.3 %prepare.1 = (f32[64,4,128]{2,1,0:T(4,128)S(1)}, s32[1,256]{1,0:T(1,128)S(1)}, s32[8,128]{1,0:T(8,128)S(1)}, bf16[1792,256]{1,0:T(8,128)(2,1)S(1)}, f32[1792,128]{1,0:T(8,128)S(1)}, /*index=5*/f32[1,1792,128]{2,1,0:T(8,128)}) custom-call(s32[2,2,64]{2,1,0:T(2,128)} %bitcast.5, bf16[2,1,1792,128]{3,2,1,0:T(8,128)(2,1)} %grads.3, f32[1,1792,128]{2,1,0:T(8,128)} %error.3, ...), custom_call_target="tpu_custom_call" | custom-call | tf_op jit(solution)/shard_map/prepare/pallas_call | solution.py:139
  3.9 28.1 %all_to_all.5 = f32[64,4,128]{2,1,0:T(4,128)S(1)} all-to-all(f32[64,4,128]{2,1,0:T(4,128)S(1)} %get-tuple-element.14), channel_id=1, replica_groups={{400,408,416,424,432,440,448,456,464,472,480,488,496,504,0,8,16,24,32,4..., dimensions={0} | all-to-all | bytes 262144 | tf_op jit(solution)/shard_map/all_to_all | solution.py:283
  32.0 1.5 %finish.1 = (f32[1,1792,128]{2,1,0:T(8,128)}, f32[1792,128]{1,0:T(8,128)}) custom-call(s32[1,256]{1,0:T(1,128)S(1)} %get-tuple-element.10.order, s32[8,128]{1,0:T(8,128)S(1)} %get-tuple-element.11.own, bf16[1792,256]{1,0:T(8,128)(2,1)S(1)} %get-tuple-element.12.hot, f32[1792,128]{1,0:T(8,128)S(1)} %get-tuple-element.13.held, ...), custom_call_target="tpu_custom_call", output_to_operand_aliasing={{0}: (8, {})} | custom-call | tf_op jit(solution)/shard_map/finish/pallas_call | solution.py:247

commit v11 on v10

--- a/solution.py
+++ b/solution.py
@@ -1,5 +1,3 @@
-import functools
-
 import jax
 import jax.numpy as jnp
 from jax import lax
@@ -12,8 +10,7 @@
 BLOCK = 128
 SENT = STEPS * PICKS
 WIDE = 4
-FIRST_Z = 12
-FIRST_X = 2
+FIRST = 11 * WIDE + 2
 EARLY_Z = 5
 EARLY_TILES = (256,) * 7
 F_ROWS = 8
@@ -89,9 +86,11 @@
     for j in range(SENT):
         own[pl.ds(j, 1), :] = jnp.full((1, BLOCK), chosen[j], jnp.int32)
     scan.wait()
-    order[...] = jnp.concatenate(
-        [lanes[j // PICKS, pl.ds(j % PICKS, 1), :] for j in range(SENT)], axis=1
-    )
+    parts = []
+    for j in range(SENT):
+        lane = lanes[j // PICKS, pl.ds(j % PICKS, 1), :]
+        parts += [lane[:, FIRST:], lane[:, :FIRST]]
+    order[...] = jnp.concatenate(parts, axis=1)
     for load in loads:
         load.wait()
 
@@ -166,18 +165,18 @@
 
 
 def finish_kernel(
-    members, order, own, hot, held, rows, grads, error, accum, _,
-    error_out, accum_out, turned, steps, errors, sums, sems,
+    order, own, hot, held, rows, grads, error, accum, _,
+    error_out, accum_out, steps, errors, sums, sems,
 ):
     replica = lax.axis_index("rep")
     tiles = sems.shape[1]
     size = sums.shape[0] // tiles
-    count = len(members)
+    count = rows.shape[0] // SENT
 
     def split_rows():
-        for place, owner in enumerate(members):
-            turned[pl.ds(owner, SENT, count), :] = rows[pl.ds(place * SENT, SENT), :]
-        value = turned[...]
+        value = jnp.concatenate(
+            [rows[pl.ds(j, count, SENT), :] for j in range(SENT)], axis=0
+        )
         high = value.astype(jnp.bfloat16)
         low = (value - high.astype(jnp.float32)).astype(jnp.bfloat16)
         return jnp.concatenate([high, low], axis=1)
@@ -243,9 +242,9 @@
             store.wait()
 
 
-def finish(members, order, own, hot, held, rows, grads, error, accum, done, tiles=7):
+def finish(order, own, hot, held, rows, grads, error, accum, done, tiles=7):
     return pl.pallas_call(
-        functools.partial(finish_kernel, members),
+        finish_kernel,
         out_shape=(
             pltpu.HBM(error.shape, jnp.float32),
             pltpu.HBM(accum.shape, jnp.float32),
@@ -258,7 +257,6 @@
         ),
         input_output_aliases={8: 0},
         scratch_shapes=[
-            pltpu.VMEM(rows.shape, jnp.float32),
             pltpu.VMEM((STEPS,) + accum.shape, jnp.bfloat16),
             pltpu.VMEM(accum.shape, jnp.float32),
             pltpu.VMEM(accum.shape, jnp.float32),
@@ -270,8 +268,7 @@
 
 
 def exchange_order(count):
-    first = FIRST_Z * WIDE + FIRST_X
-    return [(first + place) % count for place in range(count)]
+    return [(FIRST + place) % count for place in range(count)]
 
 
 def local(grads, error_in, accum_in, picks):
@@ -285,7 +282,7 @@
     )
     rows = rows.reshape(count * SENT, BLOCK)
     error, accum = finish(
-        members, order, own, hot, held, rows, grads, error_in, accum_in, in_hbm(done)
+        order, own, hot, held, rows, grads, error_in, accum_in, in_hbm(done)
     )
     return (accum, error)
 

time: 33.8 us -> 32.3 us (0.956)
  blocking collectives: 28.1 us -> 26.7 us
    all_to_all x1, blocking collectives: 28.1 us -> 26.7 us  [local(): lax.all_to_all(rows, 'rep', 0, 0, axis_index_groups=[members], tiled=True)]
where the time goes in v11:
time: 32.3 us; the launch traced here: 32.1 us
  blocking collectives  26.7 us (83%)
  Pallas kernels  4.75 us (15%)
  between operations  0.64 us (2%)
    all_to_all x1, blocking collectives, local(): lax.all_to_all(rows, 'rep', 0, 0, axis_index_groups=[members], tiled=True)  26.7 us
    pallas_call x1, Pallas kernels, prepare(): pl.pallas_call(prepare_kernel, out_shape=(pltpu.VMEM((count, SENT, BLOCK)...  3.29 us
    pallas_call x1, Pallas kernels, finish(): pl.pallas_call(finish_kernel, out_shape=(pltpu.HBM(error.shape, jnp.float...  1.46 us

profile of v11, /device:TPU:24, one launch (start us, length us, event | category | flops | bytes accessed | tf_op | source)
XLA Modules:
  0.0 32.1 jit_solution(18374411930015652977)
XLA Ops:
  0.6 3.3 %prepare.1 = (f32[64,4,128]{2,1,0:T(4,128)S(1)}, s32[1,256]{1,0:T(1,128)S(1)}, s32[8,128]{1,0:T(8,128)S(1)}, bf16[1792,256]{1,0:T(8,128)(2,1)S(1)}, f32[1792,128]{1,0:T(8,128)S(1)}, /*index=5*/f32[1,1792,128]{2,1,0:T(8,128)}) custom-call(s32[2,2,64]{2,1,0:T(2,128)} %bitcast.5, bf16[2,1,1792,128]{3,2,1,0:T(8,128)(2,1)} %grads.3, f32[1,1792,128]{2,1,0:T(8,128)} %error.3, ...), custom_call_target="tpu_custom_call" | custom-call | tf_op jit(solution)/shard_map/prepare/pallas_call | solution.py:138
  3.9 26.7 %all_to_all.5 = f32[64,4,128]{2,1,0:T(4,128)S(1)} all-to-all(f32[64,4,128]{2,1,0:T(4,128)S(1)} %get-tuple-element.14), channel_id=1, replica_groups={{368,376,384,392,400,408,416,424,432,440,448,456,464,472,480,488,496,50..., dimensions={0} | all-to-all | bytes 262144 | tf_op jit(solution)/shard_map/all_to_all | solution.py:280
  30.6 1.5 %finish.1 = (f32[1,1792,128]{2,1,0:T(8,128)}, f32[1792,128]{1,0:T(8,128)}) custom-call(s32[1,256]{1,0:T(1,128)S(1)} %get-tuple-element.10.order, s32[8,128]{1,0:T(8,128)S(1)} %get-tuple-element.11.own, bf16[1792,256]{1,0:T(8,128)(2,1)S(1)} %get-tuple-element.12.hot, f32[1792,128]{1,0:T(8,128)S(1)} %get-tuple-element.13.held, ...), custom_call_target="tpu_custom_call", output_to_operand_aliasing={{0}: (8, {})} | custom-call | tf_op jit(solution)/shard_map/finish/pallas_call | solution.py:246

commit v12 on v11

--- a/solution.py
+++ b/solution.py
@@ -115,21 +115,26 @@
         hold.start()
         tiles = store_sems.shape[0]
         size = errors.shape[0] // tiles
-        stores = []
-        for tile in range(tiles):
-            part = pl.ds(tile * size, size)
+
+        def store(tile):
+            part = pl.ds(pl.multiple_of(tile * size, size), size)
+            return pltpu.make_async_copy(
+                errors.at[part, :], error_out.at[0, part, :], store_sems.at[tile]
+            )
+
+        @pl.loop(0, tiles)
+        def _(tile):
+            part = pl.ds(pl.multiple_of(tile * size, size), size)
             hot[part, :] = one_hot(order[...], tile * size, size)
             pair = [steps[step, part, :] for step in range(STEPS)]
             errors[part, :] = tile_error(pair, errors[part, :], chosen, tile * size)
-            stores.append(
-                pltpu.make_async_copy(
-                    errors.at[part, :], error_out.at[0, part, :], store_sems.at[tile]
-                )
-            )
-            stores[-1].start()
+            store(tile).start()
+
         hold.wait()
-        for store in stores:
-            store.wait()
+
+        @pl.loop(0, tiles)
+        def _(tile):
+            store(tile).wait()
 
 
 def prepare(picks, grads, error, accum, chunks=4, tiles=7):
@@ -206,40 +211,48 @@
 
     @pl.when(jnp.logical_not(early))
     def _():
-        loads, stores = [], []
-        for tile in range(tiles):
-            part = pl.ds(tile * size, size)
-            loads.append((
-                pltpu.make_async_copy(
-                    accum.at[part, :], sums.at[part, :], sems.at[1, tile]
-                ),
-                pltpu.make_async_copy(
-                    grads.at[:, 0, part, :], steps.at[:, part, :], sems.at[2, tile]
-                ),
-                pltpu.make_async_copy(
-                    error.at[0, part, :], errors.at[part, :], sems.at[3, tile]
-                ),
-            ))
-            for load in loads[-1]:
+        def moves(tile):
+            part = pl.ds(pl.multiple_of(tile * size, size), size)
+            loads = (
+                (accum.at[part, :], sums.at[part, :]),
+                (grads.at[:, 0, part, :], steps.at[:, part, :]),
+                (error.at[0, part, :], errors.at[part, :]),
+            )
+            stores = (
+                (sums.at[part, :], accum_out.at[part, :]),
+                (errors.at[part, :], error_out.at[0, part, :]),
+            )
+            made = [
+                pltpu.make_async_copy(*pair, sems.at[place, tile])
+                for place, pair in enumerate(loads + stores)
+            ]
+            return part, made[:3], made[3:]
+
+        @pl.loop(0, tiles)
+        def _(tile):
+            for load in moves(tile)[1]:
                 load.start()
+
         pair = split_rows()
         mine = [own[pl.ds(j, 1), :] for j in range(SENT)]
-        for tile in range(tiles):
-            part = pl.ds(tile * size, size)
+
+        @pl.loop(0, tiles)
+        def _(tile):
+            part, loads, stores = moves(tile)
             hot_tile = one_hot(order[...], tile * size, size)
-            for load in loads[tile]:
+            for load in loads:
                 load.wait()
-            stores.append(store_sum(tile, part, hot_tile, pair, sums[part, :]))
+            both = jnp.dot(hot_tile, pair, preferred_element_type=jnp.float32)
+            sums[part, :] += both[:, :BLOCK] + both[:, BLOCK:]
             step_tiles = [steps[step, part, :] for step in range(STEPS)]
             errors[part, :] = tile_error(step_tiles, errors[part, :], mine, tile * size)
-            stores.append(
-                pltpu.make_async_copy(
-                    errors.at[part, :], error_out.at[0, part, :], sems.at[4, tile]
-                )
-            )
-            stores[-1].start()
-        for store in stores:
-            store.wait()
+            for store in stores:
+                store.start()
+
+        @pl.loop(0, tiles)
+        def _(tile):
+            for store in moves(tile)[2]:
+                store.wait()
 
 
 def finish(order, own, hot, held, rows, grads, error, accum, done, tiles=7):

time: 32.3 us -> 32.3 us (level)
  no operation moved by 1% of the time
where the time goes in v12:
time: 32.3 us; the launch traced here: 32.1 us
  blocking collectives  26.8 us (83%)
  Pallas kernels  4.62 us (14%)
  between operations  0.64 us (2%)
    all_to_all x1, blocking collectives, local(): lax.all_to_all(rows, 'rep', 0, 0, axis_index_groups=[members], tiled=True)  26.8 us
    pallas_call x1, Pallas kernels, prepare(): pl.pallas_call(prepare_kernel, out_shape=(pltpu.VMEM((count, SENT, BLOCK)...  3.16 us
    pallas_call x1, Pallas kernels, finish(): pl.pallas_call(finish_kernel, out_shape=(pltpu.HBM(error.shape, jnp.float...  1.46 us

profile of v12, /device:TPU:24, one launch (start us, length us, event | category | flops | bytes accessed | tf_op | source)
XLA Modules:
  0.0 32.1 jit_solution(9015849142847086406)
XLA Ops:
  0.6 3.2 %prepare.1 = (f32[64,4,128]{2,1,0:T(4,128)S(1)}, s32[1,256]{1,0:T(1,128)S(1)}, s32[8,128]{1,0:T(8,128)S(1)}, bf16[1792,256]{1,0:T(8,128)(2,1)S(1)}, f32[1792,128]{1,0:T(8,128)S(1)}, /*index=5*/f32[1,1792,128]{2,1,0:T(8,128)}) custom-call(s32[2,2,64]{2,1,0:T(2,128)} %bitcast.5, bf16[2,1,1792,128]{3,2,1,0:T(8,128)(2,1)} %grads.3, f32[1,1792,128]{2,1,0:T(8,128)} %error.3, ...), custom_call_target="tpu_custom_call" | custom-call | tf_op jit(solution)/shard_map/prepare/pallas_call | solution.py:143
  3.8 26.8 %all_to_all.5 = f32[64,4,128]{2,1,0:T(4,128)S(1)} all-to-all(f32[64,4,128]{2,1,0:T(4,128)S(1)} %get-tuple-element.14), channel_id=1, replica_groups={{368,376,384,392,400,408,416,424,432,440,448,456,464,472,480,488,496,50..., dimensions={0} | all-to-all | bytes 262144 | tf_op jit(solution)/shard_map/all_to_all | solution.py:293
  30.6 1.5 %finish.1 = (f32[1,1792,128]{2,1,0:T(8,128)}, f32[1792,128]{1,0:T(8,128)}) custom-call(s32[1,256]{1,0:T(1,128)S(1)} %get-tuple-element.10.order, s32[8,128]{1,0:T(8,128)S(1)} %get-tuple-element.11.own, bf16[1792,256]{1,0:T(8,128)(2,1)S(1)} %get-tuple-element.12.hot, f32[1792,128]{1,0:T(8,128)S(1)} %get-tuple-element.13.held, ...), custom_call_target="tpu_custom_call", output_to_operand_aliasing={{0}: (8, {})} | custom-call | tf_op jit(solution)/shard_map/finish/pallas_call | solution.py:259
